TPU v7x, 32 devices: a whole 2x2x4 slice. The times are simulated.
32 devices in a mesh: seq: 16 (over z, y, core), cp: 2 (over x).
Axes of the slice: x: 2, y: 2, z: 4, core: 2. Of those that a mesh axis runs over, the one named last changes fastest.
Arguments:
- inputs: bfloat16 [16384, 768], P(('seq', 'cp')), may hold values from -6 to 6
- doc_ids: int32 [16384], P(('seq', 'cp')), may hold values from 0 to 5, as said below
- cotangent: bfloat16 [16384, 768], P(('seq', 'cp')), may hold values from -6 to 6
- attn_norm_gain: bfloat16 [2, 768], P(None, ('seq', 'cp')), may hold values from 0.5 to 1.5
- attn_norm_bias: bfloat16 [2, 768], P(None, ('seq', 'cp')), may hold values from -1 to 1
- mlp_norm_gain: bfloat16 [2, 768], P(None, ('seq', 'cp')), may hold values from 0.5 to 1.5
- mlp_norm_bias: bfloat16 [2, 768], P(None, ('seq', 'cp')), may hold values from -1 to 1
- qkv_weight: bfloat16 [2, 768, 2304], P(None, ('seq', 'cp')), may hold values from -0.21875 to 0.21875
- qkv_bias: bfloat16 [2, 2304], P(None, ('seq', 'cp')), may hold values from -1 to 1
- dense_weight: bfloat16 [2, 768, 768], P(None, ('seq', 'cp')), may hold values from -1.25 to 1.25
- dense_bias: bfloat16 [2, 768], P(None, ('seq', 'cp')), may hold values from -1 to 1
- up_weight: bfloat16 [2, 768, 3072], P(None, ('seq', 'cp')), may hold values from -0.21875 to 0.21875
- up_bias: bfloat16 [2, 3072], P(None, ('seq', 'cp')), may hold values from -1 to 1
- down_weight: bfloat16 [2, 3072, 768], P(None, ('seq', 'cp')), may hold values from -0.109375 to 0.109375
- down_bias: bfloat16 [2, 768], P(None, ('seq', 'cp')), may hold values from -1 to 1
Outputs:
- layer_output: bfloat16 [16384, 768], P(('seq', 'cp'))
- input_grad: float32 [16384, 768], P(('seq', 'cp'))
- grad_attn_norm_gain: float32 [2, 768], P(None, ('seq', 'cp'))
- grad_attn_norm_bias: float32 [2, 768], P(None, ('seq', 'cp'))
- grad_mlp_norm_gain: float32 [2, 768], P(None, ('seq', 'cp'))
- grad_mlp_norm_bias: float32 [2, 768], P(None, ('seq', 'cp'))
- grad_qkv_weight: float32 [2, 768, 2304], P(None, ('seq', 'cp'))
- grad_qkv_bias: float32 [2, 2304], P(None, ('seq', 'cp'))
- grad_dense_weight: float32 [2, 768, 768], P(None, ('seq', 'cp'))
- grad_dense_bias: float32 [2, 768], P(None, ('seq', 'cp'))
- grad_up_weight: float32 [2, 768, 3072], P(None, ('seq', 'cp'))
- grad_up_bias: float32 [2, 3072], P(None, ('seq', 'cp'))
- grad_down_weight: float32 [2, 3072, 768], P(None, ('seq', 'cp'))
- grad_down_bias: float32 [2, 768], P(None, ('seq', 'cp'))
Inputs may be any that keep to these rules, and one draw needn't show every extreme that they name: `doc_ids`: along each pack of 1024 tokens the numbers start at 0 and never fall; one document starts within the pack's first 512 tokens and ends within its last 512.
All inputs are finite; a program needn't handle non-finite values.
Results may differ from a plain program's by a relative error of at most 0.02.
Values may be sent and summed in bfloat16 or wider, within the bound.
No kernel may reach another device: no remote copies, remote signals or barrier semaphores. Data moves between devices by JAX's collectives and lax.ppermute only.
A program may use at most 320 MiB of HBM per device.

v0:
```python
import jax
import jax.numpy as jnp
from jax import lax
from jax.sharding import PartitionSpec as P

HEADS = 12
HEAD_DIM = 64
ROT_DIM = 16
LAYERS = 2


EPSILON = 1e-05
MASKED = -1e30


def normalize(hidden):
    average = jnp.mean(hidden, axis=-1, keepdims=True)
    centered = hidden - average
    variance = jnp.mean(centered * centered, axis=-1, keepdims=True)
    inverse_std = lax.rsqrt(variance + EPSILON)
    return (centered * inverse_std, inverse_std)


def rotary_tables(positions):
    half_rot = ROT_DIM // 2
    inverse = 10000.0 ** (-(jnp.arange(half_rot, dtype=jnp.float32) * 2.0 / ROT_DIM))
    angles = positions.astype(jnp.float32)[:, None] * jnp.concatenate([inverse, inverse])[None, :]
    return (jnp.cos(angles), jnp.sin(angles))


def rotate(vectors, cosine, sine_table):
    half_rot = ROT_DIM // 2
    turned = vectors[:, :, :ROT_DIM]
    swapped = jnp.concatenate([-turned[:, :, half_rot:], turned[:, :, :half_rot]], axis=2)
    rotated = turned * cosine[:, None, :] + swapped * sine_table[:, None, :]
    return jnp.concatenate([rotated, vectors[:, :, ROT_DIM:]], axis=2)


def unrotate(incoming, cosine, sine_table):
    half_rot = ROT_DIM // 2
    turned = incoming[:, :, :ROT_DIM]
    sine_part = turned * sine_table[:, None, :]
    back_part = jnp.concatenate([sine_part[:, :, half_rot:], -sine_part[:, :, :half_rot]], axis=2)
    rotated = turned * cosine[:, None, :] + back_part
    return jnp.concatenate([rotated, incoming[:, :, ROT_DIM:]], axis=2)


def contract_rows(left_side, right_side):
    return lax.dot_general(
        left_side, right_side, (((0,), (0,)), ((), ())), preferred_element_type=jnp.float32
    )


def times_transposed(left_side, right_side):
    return lax.dot_general(
        left_side, right_side, (((1,), (1,)), ((), ())), preferred_element_type=jnp.float32
    )


def split_blocks(tensor):
    total_rows = tensor.shape[0]
    block_width = min(512, total_rows)
    return tensor.reshape((total_rows // block_width, block_width) + tensor.shape[1:])


def owner_rows(members, owners):
    return jnp.concatenate([member.reshape(owners, -1) for member in members], axis=1)


def unpack_rows(flat_share, members, owners):
    results = []
    offset = 0
    for member in members:
        width = member.size // owners
        piece = flat_share[offset : offset + width]
        results.append(piece.reshape((member.shape[0] // owners,) + member.shape[1:]))
        offset = offset + width
    return results


def masked_scores(queries, block_keys, block_docs, block_place, row_docs, row_place):
    scores = jnp.einsum(
        "qhd,khd->hqk", queries, block_keys, preferred_element_type=jnp.float32
    ) * HEAD_DIM ** (-0.5)
    allowed = (block_place[None, :] <= row_place[:, None]) & (
        block_docs[None, :] == row_docs[:, None]
    )
    return (jnp.where(allowed[None], scores, MASKED), allowed)


def key_block_tuple(all_keys, all_values, key_docs):
    key_place = jnp.arange(all_keys.shape[0], dtype=jnp.int32)
    return (
        split_blocks(all_keys),
        split_blocks(all_values),
        split_blocks(key_docs),
        split_blocks(key_place),
    )


def attend_forward(queries, all_keys, all_values, key_docs, row_docs, row_place):
    blocks = key_block_tuple(all_keys, all_values, key_docs)
    heads_count = queries.shape[1]
    row_count = queries.shape[0]

    def stats_step(running, block_item):
        running_max, running_sum = running
        scores, allowed = masked_scores(
            queries, block_item[0], block_item[2], block_item[3], row_docs, row_place
        )
        new_max = jnp.maximum(running_max, jnp.max(scores, axis=-1))
        exp_terms = jnp.where(allowed[None], jnp.exp(scores - new_max[:, :, None]), 0.0)
        new_sum = running_sum * jnp.exp(running_max - new_max) + jnp.sum(exp_terms, axis=-1)
        return ((new_max, new_sum), None)

    initial = (
        jnp.full((heads_count, row_count), MASKED, jnp.float32),
        jnp.zeros((heads_count, row_count), jnp.float32),
    )
    (row_max, row_sum), unused = lax.scan(stats_step, initial, blocks)

    def output_step(running_total, block_item):
        scores, allowed = masked_scores(
            queries, block_item[0], block_item[2], block_item[3], row_docs, row_place
        )
        probabilities = (jnp.exp(scores - row_max[:, :, None]) / row_sum[:, :, None]).astype(
            jnp.bfloat16
        )
        added = jnp.einsum(
            "hqk,khd->qhd", probabilities, block_item[1], preferred_element_type=jnp.float32
        )
        return (running_total + added, None)

    output, unused = lax.scan(output_step, jnp.zeros(queries.shape, jnp.float32), blocks)
    return (output, row_max, row_sum)


def attend_backward(
    queries,
    all_keys,
    all_values,
    key_docs,
    row_docs,
    row_place,
    row_max,
    row_sum,
    grad_attended,
    row_delta,
):
    blocks = key_block_tuple(all_keys, all_values, key_docs)
    scale_factor = HEAD_DIM ** (-0.5)

    def grad_step(grad_queries, block_item):
        scores, allowed = masked_scores(
            queries, block_item[0], block_item[2], block_item[3], row_docs, row_place
        )
        probabilities = jnp.exp(scores - row_max[:, :, None]) / row_sum[:, :, None]
        grad_probs = jnp.einsum(
            "qhd,khd->hqk", grad_attended, block_item[1], preferred_element_type=jnp.float32
        )
        grad_scores = (probabilities * (grad_probs - row_delta[:, :, None])).astype(jnp.bfloat16)
        grad_queries = (
            grad_queries
            + jnp.einsum(
                "hqk,khd->qhd", grad_scores, block_item[0], preferred_element_type=jnp.float32
            )
            * scale_factor
        )
        grad_keys = (
            jnp.einsum("hqk,qhd->khd", grad_scores, queries, preferred_element_type=jnp.float32)
            * scale_factor
        )
        grad_values = jnp.einsum(
            "hqk,qhd->khd",
            probabilities.astype(jnp.bfloat16),
            grad_attended,
            preferred_element_type=jnp.float32,
        )
        return (grad_queries, (grad_keys, grad_values))

    grad_queries, (grad_keys, grad_values) = lax.scan(
        grad_step, jnp.zeros(queries.shape, jnp.float32), blocks
    )
    total_keys = all_keys.shape[0]
    return (grad_queries, grad_keys.reshape(total_keys, -1), grad_values.reshape(total_keys, -1))


def fetch_forward(params, layer_index):
    (
        gain_attn,
        bias_attn,
        gain_mlp,
        bias_mlp,
        qkv_weight,
        qkv_bias,
        dense_weight,
        dense_bias,
        up_weight,
        up_bias,
        down_weight,
        down_bias,
    ) = params
    return (
        lax.all_gather(gain_attn[layer_index], ("seq", "cp"), axis=0, tiled=True),
        lax.all_gather(bias_attn[layer_index], ("seq", "cp"), axis=0, tiled=True),
        lax.all_gather(gain_mlp[layer_index], ("seq", "cp"), axis=0, tiled=True),
        lax.all_gather(bias_mlp[layer_index], ("seq", "cp"), axis=0, tiled=True),
        lax.all_gather(qkv_weight[layer_index], ("seq", "cp"), axis=0, tiled=True),
        lax.all_gather(qkv_bias[layer_index], ("seq", "cp"), axis=0, tiled=True),
        lax.all_gather(dense_weight[layer_index], ("seq", "cp"), axis=0, tiled=True),
        lax.all_gather(dense_bias[layer_index], ("seq", "cp"), axis=0, tiled=True),
        lax.all_gather(up_weight[layer_index], ("seq", "cp"), axis=0, tiled=True),
        lax.all_gather(up_bias[layer_index], ("seq", "cp"), axis=0, tiled=True),
        lax.all_gather(down_weight[layer_index], ("seq", "cp"), axis=0, tiled=True),
        lax.all_gather(down_bias[layer_index], ("seq", "cp"), axis=0, tiled=True),
    )


def fetch_backward(params, layer_index):
    (
        gain_attn,
        bias_attn,
        gain_mlp,
        bias_mlp,
        qkv_weight,
        qkv_bias,
        dense_weight,
        dense_bias,
        up_weight,
        up_bias,
        down_weight,
        down_bias,
    ) = params
    return (
        lax.all_gather(gain_attn[layer_index], ("seq", "cp"), axis=0, tiled=True),
        lax.all_gather(bias_attn[layer_index], ("seq", "cp"), axis=0, tiled=True),
        lax.all_gather(gain_mlp[layer_index], ("seq", "cp"), axis=0, tiled=True),
        lax.all_gather(bias_mlp[layer_index], ("seq", "cp"), axis=0, tiled=True),
        lax.all_gather(qkv_weight[layer_index], ("seq", "cp"), axis=0, tiled=True),
        lax.all_gather(qkv_bias[layer_index], ("seq", "cp"), axis=0, tiled=True),
        lax.all_gather(dense_weight[layer_index], ("seq", "cp"), axis=0, tiled=True),
        lax.all_gather(dense_bias[layer_index], ("seq", "cp"), axis=0, tiled=True),
        lax.all_gather(up_weight[layer_index], ("seq", "cp"), axis=0, tiled=True),
        lax.all_gather(up_bias[layer_index], ("seq", "cp"), axis=0, tiled=True),
        lax.all_gather(down_weight[layer_index], ("seq", "cp"), axis=0, tiled=True),
        lax.all_gather(down_bias[layer_index], ("seq", "cp"), axis=0, tiled=True),
    )


def layer_forward(hidden, weights, cosine, sine_table, key_docs, row_docs, row_place):
    (
        gain_attn,
        bias_attn,
        gain_mlp,
        bias_mlp,
        qkv_weight,
        qkv_bias,
        dense_weight,
        dense_bias,
        up_weight,
        up_bias,
        down_weight,
        down_bias,
    ) = weights
    row_count = hidden.shape[0]
    normed, inverse_std = normalize(hidden)
    attn_in = (normed * gain_attn.astype(jnp.float32) + bias_attn.astype(jnp.float32)).astype(
        jnp.bfloat16
    )
    mlp_in = (normed * gain_mlp.astype(jnp.float32) + bias_mlp.astype(jnp.float32)).astype(
        jnp.bfloat16
    )
    mixed_proj = jnp.dot(attn_in, qkv_weight, preferred_element_type=jnp.float32) + qkv_bias.astype(
        jnp.float32
    )
    shaped = mixed_proj.reshape(row_count, 3, HEADS, HEAD_DIM)
    queries = rotate(shaped[:, 0], cosine, sine_table).astype(jnp.bfloat16)
    local_keys = (
        rotate(shaped[:, 1], cosine, sine_table).astype(jnp.bfloat16).reshape(row_count, -1)
    )
    local_values = shaped[:, 2].astype(jnp.bfloat16).reshape(row_count, -1)
    all_keys, all_values = (
        lax.all_gather(local_keys, "cp", axis=0, tiled=True),
        lax.all_gather(local_values, "cp", axis=0, tiled=True),
    )
    all_keys = all_keys.reshape(-1, HEADS, HEAD_DIM)
    all_values = all_values.reshape(-1, HEADS, HEAD_DIM)
    output, row_max, row_sum = attend_forward(
        queries, all_keys, all_values, key_docs, row_docs, row_place
    )
    attended = output.reshape(row_count, -1).astype(jnp.bfloat16)
    branch_attn = jnp.dot(
        attended, dense_weight, preferred_element_type=jnp.float32
    ) + dense_bias.astype(jnp.float32)
    upper_pre = jnp.dot(mlp_in, up_weight, preferred_element_type=jnp.float32) + up_bias.astype(
        jnp.float32
    )
    activated = jax.nn.gelu(upper_pre, approximate=False).astype(jnp.bfloat16)
    branch_mlp = jnp.dot(
        activated, down_weight, preferred_element_type=jnp.float32
    ) + down_bias.astype(jnp.float32)
    result_hidden = hidden + branch_attn + branch_mlp
    forward_kept = (
        normed,
        inverse_std,
        attn_in,
        mlp_in,
        queries,
        local_keys,
        local_values,
        all_keys,
        all_values,
        output,
        row_max,
        row_sum,
        attended,
        upper_pre,
        activated,
    )
    return (result_hidden, forward_kept)


def layer_backward(
    upstream,
    weights,
    forward_kept,
    all_keys,
    all_values,
    cosine,
    sine_table,
    key_docs,
    row_docs,
    row_place,
):
    (
        gain_attn,
        bias_attn,
        gain_mlp,
        bias_mlp,
        qkv_weight,
        qkv_bias,
        dense_weight,
        dense_bias,
        up_weight,
        up_bias,
        down_weight,
        down_bias,
    ) = weights
    (
        normed,
        inverse_std,
        attn_in,
        mlp_in,
        queries,
        local_keys,
        local_values,
        kept_keys,
        kept_values,
        output,
        row_max,
        row_sum,
        attended,
        upper_pre,
        activated,
    ) = forward_kept
    row_count = upstream.shape[0]
    upstream_low = upstream.astype(jnp.bfloat16)
    grad_down = contract_rows(activated, upstream_low)
    grad_dense = contract_rows(attended, upstream_low)
    grad_out_bias = jnp.sum(upstream_low.astype(jnp.float32), axis=0)
    grad_activated = times_transposed(upstream_low, down_weight)
    unused, gelu_pull = jax.vjp(lambda values: jax.nn.gelu(values, approximate=False), upper_pre)
    grad_upper = gelu_pull(grad_activated)[0].astype(jnp.bfloat16)
    grad_up = contract_rows(mlp_in, grad_upper)
    grad_up_bias = jnp.sum(grad_upper.astype(jnp.float32), axis=0)
    grad_mlp_in = times_transposed(grad_upper, up_weight)
    grad_attended = (
        times_transposed(upstream_low, dense_weight)
        .astype(jnp.bfloat16)
        .reshape(row_count, HEADS, HEAD_DIM)
    )
    row_delta = jnp.transpose(jnp.sum(grad_attended.astype(jnp.float32) * output, axis=-1))
    grad_queries, block_grad_keys, block_grad_values = attend_backward(
        queries,
        all_keys,
        all_values,
        key_docs,
        row_docs,
        row_place,
        row_max,
        row_sum,
        grad_attended,
        row_delta,
    )
    grad_keys, grad_values = (
        lax.psum_scatter(
            block_grad_keys.astype(jnp.bfloat16), "cp", scatter_dimension=0, tiled=True
        ).astype(jnp.float32),
        lax.psum_scatter(
            block_grad_values.astype(jnp.bfloat16), "cp", scatter_dimension=0, tiled=True
        ).astype(jnp.float32),
    )
    grad_mixed = jnp.stack(
        [
            unrotate(grad_queries, cosine, sine_table),
            unrotate(grad_keys.reshape(row_count, HEADS, HEAD_DIM), cosine, sine_table),
            grad_values.reshape(row_count, HEADS, HEAD_DIM),
        ],
        axis=1,
    )
    grad_mixed = grad_mixed.reshape(row_count, -1).astype(jnp.bfloat16)
    grad_qkv = contract_rows(attn_in, grad_mixed)
    grad_qkv_bias = jnp.sum(grad_mixed.astype(jnp.float32), axis=0)
    grad_attn_in = times_transposed(grad_mixed, qkv_weight)
    grad_gain_attn = jnp.sum(grad_attn_in * normed, axis=0)
    grad_bias_attn = jnp.sum(grad_attn_in, axis=0)
    grad_gain_mlp = jnp.sum(grad_mlp_in * normed, axis=0)
    grad_bias_mlp = jnp.sum(grad_mlp_in, axis=0)
    grad_normed = grad_attn_in * gain_attn.astype(jnp.float32) + grad_mlp_in * gain_mlp.astype(
        jnp.float32
    )
    centered_grad = (
        grad_normed
        - jnp.mean(grad_normed, axis=-1, keepdims=True)
        - normed * jnp.mean(grad_normed * normed, axis=-1, keepdims=True)
    )
    grad_input = upstream + inverse_std * centered_grad
    local_grads = (
        grad_gain_attn,
        grad_bias_attn,
        grad_gain_mlp,
        grad_bias_mlp,
        grad_qkv,
        grad_qkv_bias,
        grad_dense,
        grad_out_bias,
        grad_up,
        grad_up_bias,
        grad_down,
        grad_out_bias,
    )
    return (grad_input, local_grads)


def per_device(
    inputs,
    doc_ids,
    cotangent,
    attn_norm_gain,
    attn_norm_bias,
    mlp_norm_gain,
    mlp_norm_bias,
    qkv_weight,
    qkv_bias,
    dense_weight,
    dense_bias,
    up_weight,
    up_bias,
    down_weight,
    down_bias,
):
    params = (
        attn_norm_gain,
        attn_norm_bias,
        mlp_norm_gain,
        mlp_norm_bias,
        qkv_weight,
        qkv_bias,
        dense_weight,
        dense_bias,
        up_weight,
        up_bias,
        down_weight,
        down_bias,
    )
    row_count = inputs.shape[0]
    owners = lax.axis_size(("seq", "cp"))
    key_docs = lax.all_gather(doc_ids, "cp", axis=0, tiled=True)
    row_place = lax.axis_index("cp") * row_count + jnp.arange(row_count, dtype=jnp.int32)
    starts = jnp.sum((key_docs[None, :] < doc_ids[:, None]).astype(jnp.int32), axis=1)
    cosine, sine_table = rotary_tables(row_place - starts)
    hidden = inputs.astype(jnp.float32)
    records = []
    for layer_index in range(LAYERS):
        weights = fetch_forward(params, layer_index)
        hidden, forward_kept = layer_forward(
            hidden, weights, cosine, sine_table, key_docs, doc_ids, row_place
        )
        records.append((weights, forward_kept))
    upstream = cotangent.astype(jnp.float32)
    per_layer = [None] * LAYERS
    full_layers = [None] * LAYERS
    for layer_index in reversed(range(LAYERS)):
        weights, forward_kept = records[layer_index]
        weights = fetch_backward(params, layer_index)
        all_keys, all_values = (
            lax.all_gather(forward_kept[5], "cp", axis=0, tiled=True),
            lax.all_gather(forward_kept[6], "cp", axis=0, tiled=True),
        )
        all_keys = all_keys.reshape(-1, HEADS, HEAD_DIM)
        all_values = all_values.reshape(-1, HEADS, HEAD_DIM)
        upstream, local_grads = layer_backward(
            upstream,
            weights,
            forward_kept,
            all_keys,
            all_values,
            cosine,
            sine_table,
            key_docs,
            doc_ids,
            row_place,
        )
        full_layers[layer_index] = local_grads
        flat_terms = owner_rows(local_grads, owners).reshape(-1)
        flat_share = lax.psum_scatter(flat_terms, ("seq", "cp"), scatter_dimension=0, tiled=True)
        per_layer[layer_index] = unpack_rows(flat_share, local_grads, owners)
    stacked = tuple(
        (
            jnp.stack([per_layer[position][member] for position in range(LAYERS)])
            for member in range(12)
        )
    )
    return (
        hidden.astype(jnp.bfloat16),
        upstream,
        stacked[0],
        stacked[1],
        stacked[2],
        stacked[3],
        stacked[4],
        stacked[5],
        stacked[6],
        stacked[7],
        stacked[8],
        stacked[9],
        stacked[10],
        stacked[11],
    )


def solution(mesh):
    return jax.shard_map(
        per_device,
        mesh=mesh,
        in_specs=(
            P(("seq", "cp"), None),
            P(("seq", "cp")),
            P(("seq", "cp"), None),
            P(None, ("seq", "cp")),
            P(None, ("seq", "cp")),
            P(None, ("seq", "cp")),
            P(None, ("seq", "cp")),
            P(None, ("seq", "cp"), None),
            P(None, ("seq", "cp")),
            P(None, ("seq", "cp"), None),
            P(None, ("seq", "cp")),
            P(None, ("seq", "cp"), None),
            P(None, ("seq", "cp")),
            P(None, ("seq", "cp"), None),
            P(None, ("seq", "cp")),
        ),
        out_specs=(
            P(("seq", "cp"), None),
            P(("seq", "cp"), None),
            P(None, ("seq", "cp")),
            P(None, ("seq", "cp")),
            P(None, ("seq", "cp")),
            P(None, ("seq", "cp")),
            P(None, ("seq", "cp"), None),
            P(None, ("seq", "cp")),
            P(None, ("seq", "cp"), None),
            P(None, ("seq", "cp")),
            P(None, ("seq", "cp"), None),
            P(None, ("seq", "cp")),
            P(None, ("seq", "cp"), None),
            P(None, ("seq", "cp")),
        ),
        check_vma=False,
    )
```

profile of v0, /device:TPU:1, one launch (start us, length us, event | category | flops | bytes accessed | tf_op | source)
XLA Modules:
  0.0 2006.9 jit_solution(1673462510678248672)
XLA Ops:
  18.3 43.4 %all-reduce.19 = (bf16[768]{0:T(1024)(128)(2,1)}, bf16[768]{0:T(1024)(128)(2,1)}, bf16[768]{0:T(1024)(128)(2,1)S(1)}, bf16[768]{0:T(1024)(128)(2,1)S(1)}, bf16[3...) all-reduce(bf16[768]{0:T(1024)(128)(2,1)S(1)} %dynamic-update-slice, ...), channel_id=21, replica_groups=mesh['seq'=16,'cp'=2] {'seq','cp'}, use_global_device_ids=true, to_apply=%add.13 | all-reduce | flops 19968 | bytes 79872
  119.7 25.0 %all-gather.40.cloned.1.call-done = bf16[1024,768]{0,1:T(8,128)(2,1)} async-done(((bf16[512,768]{0,1:T(8,128)(2,1)}), bf16[1024,768]{0,1:T(8,128)(2,1)}) %all-gather.40.cloned.1.call-update) | async-done | bytes 1572880 | tf_op jit(solution)/shard_map/all_gather | solution.py:283
  150.2 27.1 %while.78 = (s32[]{:T(128)}, f32[12,512]{1,0:T(8,128)S(1)}, f32[12,512]{1,0:T(8,128)S(1)}, s32[2,512]{1,0:T(2,128)S(1)}, s32[2,512]{1,0:T(2,128)S(1)}, /*index=5...) while((s32[]{:T(128)}, f32[12,512]{1,0:T(8,128)S(1)}, ...), condition=%wide.region_6.7_spmd.clone, body=%wide.region_3.6_spmd.clone.sunk | while | flops 428636672 | bytes 27863180 | solution.py:120
  212.2 20.2 %multiply_convert_fusion.1 = (bf16[512,3072]{1,0:T(8,128)(2,1)}, f32[512,3072]{1,0:T(8,128)}, f32[512,3072]{1,0:T(8,128)}) fusion(f32[3072]{0:T(1024)S(1)} %convert_element_type.304, bf16[1,768,3072]{2,1,0:T(8,128)(2,1)} %all-gather.50.cloned.1.call-done, bf16[512,768]{1,0:T(8,128)(2,1)S(1)} %copy-done.13, f32[768]{0:T(1024)S(1)} %convert_element_type.303, ...), kind=kOutput, calls=%fused_computation.141 | convolution fusion | flops 2522087424 | bytes 21256192 | tf_op jit(solution)/shard_map/dot_general | solution.py:295
  232.4 45.6 %all-gather.52.cloned.1.call-done = bf16[1,3072,768]{2,1,0:T(8,128)(2,1)} async-done(((bf16[1,96,768]{2,1,0:T(8,128)(2,1)}), bf16[1,3072,768]{2,1,0:T(8,128)(2,1)}) %all-gather.52.cloned.1.call-update) | async-done | bytes 4718608 | tf_op jit(solution)/shard_map/all_gather | solution.py:214
  285.1 48.7 %all-gather.48.cloned.1.call-done = bf16[1,768,768]{2,1,0:T(8,128)(2,1)} async-done(((bf16[1,24,768]{2,1,0:T(8,128)(2,1)}), bf16[1,768,768]{2,1,0:T(8,128)(2,1)}) %all-gather.48.cloned.1.call-update) | async-done | bytes 1179664 | tf_op jit(solution)/shard_map/all_gather | solution.py:210
  336.9 58.9 %all-gather.54.cloned.1.call-done = bf16[1,768,2304]{2,1,0:T(8,128)(2,1)} async-done(((bf16[1,24,2304]{2,1,0:T(8,128)(2,1)}), bf16[1,768,2304]{2,1,0:T(8,128)(2,1)}) %all-gather.54.cloned.1.call-update) | async-done | bytes 3538960 | tf_op jit(solution)/shard_map/all_gather | solution.py:208
  416.7 35.0 %all-gather.56.cloned.1.call-done = bf16[1,768,768]{2,1,0:T(8,128)(2,1)} async-done(((bf16[1,24,768]{2,1,0:T(8,128)(2,1)}), bf16[1,768,768]{2,1,0:T(8,128)(2,1)}) %all-gather.56.cloned.1.call-update) | async-done | bytes 1179664 | tf_op jit(solution)/shard_map/all_gather | solution.py:210
  455.5 23.5 %all-gather.42.cloned.1.call-done = bf16[1024,768]{0,1:T(8,128)(2,1)} async-done(((bf16[512,768]{0,1:T(8,128)(2,1)}), bf16[1024,768]{0,1:T(8,128)(2,1)}) %all-gather.42.cloned.1.call-update) | async-done | bytes 1572880 | tf_op jit(solution)/shard_map/all_gather | solution.py:284
  485.9 21.7 %all-gather.44.cloned.1.call-done = bf16[1024,768]{0,1:T(8,128)(2,1)} async-done(((bf16[512,768]{0,1:T(8,128)(2,1)}), bf16[1024,768]{0,1:T(8,128)(2,1)}) %all-gather.44.cloned.1.call-update) | async-done | bytes 1572880 | tf_op jit(solution)/shard_map/all_gather | solution.py:283
  514.4 29.4 %while.80 = (s32[]{:T(128)}, f32[12,512]{1,0:T(8,128)S(1)}, f32[12,512]{1,0:T(8,128)S(1)}, s32[2,512]{1,0:T(2,128)S(1)}, s32[2,512]{1,0:T(2,128)S(1)}, /*index=5...) while((s32[]{:T(128)}, f32[12,512]{1,0:T(8,128)S(1)}, ...), condition=%wide.region_14.15_spmd.clone, body=%wide.region_11.14_spmd.clone.sunk | while | flops 428636672 | bytes 27863180 | solution.py:120
  564.8 54.4 %while.82 = (s32[]{:T(128)}, f32[512,12,64]{0,2,1:T(8,128)}, bf16[2,512,12,64]{1,3,2,0:T(8,128)(2,1)}, bf16[2,512,12,64]{1,3,2,0:T(8,128)(2,1)}, bf16[2,512,12,6...) while((s32[]{:T(128)}, f32[512,12,64]{0,2,1:T(8,128)}, ...), condition=%wide.region_19.20_spmd.clone, body=%wide.region_18.19_spmd.clone.sunk | while | flops 2040791552 | bytes 201165104 | solution.py:181
  627.5 19.9 multiply_convert_fusion
  671.4 24.7 %reduce-scatter.7.cloned.1.call-done = bf16[512,768]{0,1:T(8,128)(2,1)} async-done(((bf16[1024,768]{0,1:T(8,128)(2,1)}), bf16[512,768]{0,1:T(8,128)(2,1)}) %reduce-scatter.7.cloned.1.call-update) | async-done | bytes 786448 | tf_op jit(solution)/shard_map/reduce_scatter | solution.py:399
  714.4 54.1 %while.83 = (s32[]{:T(128)}, f32[512,12,64]{0,2,1:T(8,128)}, bf16[2,512,12,64]{1,3,2,0:T(8,128)(2,1)}, bf16[2,512,12,64]{1,3,2,0:T(8,128)(2,1)}, bf16[2,512,12,6...) while((s32[]{:T(128)}, f32[512,12,64]{0,2,1:T(8,128)}, ...), condition=%wide.region_26.27_spmd.clone, body=%wide.region_25.26_spmd.clone.sunk | while | flops 2040791552 | bytes 201165104 | solution.py:181
  834.7 20.5 %dynamic-update-slice.20 = f32[32,221496]{1,0:T(8,128)} dynamic-update-slice(f32[32,221496]{1,0:T(8,128)} %dynamic-update-slice.19, f32[32,55296]{1,0:T(8,128)} %reshape.687, s32[]{} %constant.281, s32[]{} %constant.285) | dynamic-update-slice | bytes 14155780
  867.5 28.7 %dynamic-update-slice.24 = f32[32,221496]{1,0:T(8,128)} dynamic-update-slice(f32[32,221496]{1,0:T(8,128)} %dynamic-update-slice.23, f32[32,73728]{1,0:T(8,128)} %reshape.691, s32[]{} %constant.281, s32[]{} %constant.289) | dynamic-update-slice | bytes 18874372
  897.8 28.3 %dynamic-update-slice.26 = f32[32,221496]{1,0:T(8,128)} dynamic-update-slice(f32[32,221496]{1,0:T(8,128)} %dynamic-update-slice.25, f32[32,73728]{1,0:T(8,128)} %reshape.693, s32[]{} %constant.281, s32[]{} %constant.291) | dynamic-update-slice | bytes 18874372
  927.7 38.5 %reshape.694 = f32[7087872]{0:T(1024)} reshape(f32[32,221496]{1,0:T(8,128)} %dynamic-update-slice.27) | data formatting | bytes 56702976 | tf_op jit(solution)/shard_map/reshape | solution.py:515
  1040.5 20.5 %dynamic-update-slice.32 = f32[32,221496]{1,0:T(8,128)} dynamic-update-slice(f32[32,221496]{1,0:T(8,128)} %dynamic-update-slice.31, f32[32,55296]{1,0:T(8,128)} %reshape.675, s32[]{} %constant.281, s32[]{} %constant.285) | dynamic-update-slice | bytes 14155780
  1073.3 28.8 %dynamic-update-slice.36 = f32[32,221496]{1,0:T(8,128)} dynamic-update-slice(f32[32,221496]{1,0:T(8,128)} %dynamic-update-slice.35, f32[32,73728]{1,0:T(8,128)} %reshape.679, s32[]{} %constant.281, s32[]{} %constant.289) | dynamic-update-slice | bytes 18874372
  1103.6 28.3 %dynamic-update-slice.38 = f32[32,221496]{1,0:T(8,128)} dynamic-update-slice(f32[32,221496]{1,0:T(8,128)} %dynamic-update-slice.37, f32[32,73728]{1,0:T(8,128)} %reshape.681, s32[]{} %constant.281, s32[]{} %constant.291) | dynamic-update-slice | bytes 18874372
  1133.5 38.0 %reshape.682 = f32[7087872]{0:T(1024)} reshape(f32[32,221496]{1,0:T(8,128)} %dynamic-update-slice.39) | data formatting | bytes 56702976 | tf_op jit(solution)/shard_map/reshape | solution.py:515
  1181.7 798.5 %all-reduce.22.cloned.1.call-done = (f32[7087872]{0:T(1024)}, f32[7087872]{0:T(1024)}) async-done(((f32[7087872]{0:T(1024)}, f32[7087872]{0:T(1024)}), (f32[7087872]{0:T(1024)}, f32[7087872]{0:T(1024)})) %all-reduce.22.cloned.1.call-update) | async-done | bytes 56702992
  (601 shorter events, 623.3 us)
Async XLA Ops:
  7.2 67.3 %all-gather.46.cloned.1.call-start = ((), (), s32[]{:S(2)}) async-start(), calls=%async_computation.12 | async-start | bytes 3649536 | tf_op jit(solution)/shard_map/all_gather | solution.py:208
  8.9 106.4 %all-gather.38.cloned.1.call-start = ((), (), s32[]{:S(2)}) async-start(), calls=%async_computation.4 | async-start | bytes 2359296 | tf_op jit(solution)/shard_map/all_gather | solution.py:284
  66.8 145.4 %copy-start.54 = (f32[512]{0:T(512)}, f32[512]{0:T(512)S(1)}, u32[]{:S(2)}) copy-start(f32[512]{0:T(512)S(1)} %broadcast_multiply_fusion.5) | copy-start | bytes 6148
  68.3 143.9 %copy-start.56 = (f32[512]{0:T(512)}, f32[512]{0:T(512)S(1)}, u32[]{:S(2)}) copy-start(f32[512]{0:T(512)S(1)} %add_rsqrt_fusion.1) | copy-start | bytes 6148
  89.7 55.0 %all-gather.40.cloned.1.call-start = ((), (), s32[]{:S(2)}) async-start(), calls=%async_computation.5 | async-start | bytes 2359296 | tf_op jit(solution)/shard_map/all_gather | solution.py:283
  94.0 118.2 %all-gather.50.cloned.1.call-start = ((), (), s32[]{:S(2)}) async-start(), calls=%async_computation.14 | async-start | bytes 4866048 | tf_op jit(solution)/shard_map/all_gather | solution.py:212
  94.8 183.2 %all-gather.52.cloned.1.call-start = ((), (), s32[]{:S(2)}) async-start(), calls=%async_computation.15 | async-start | bytes 4866048 | tf_op jit(solution)/shard_map/all_gather | solution.py:214
  96.6 237.1 %all-gather.48.cloned.1.call-start = ((), (), s32[]{:S(2)}) async-start(), calls=%async_computation.13 | async-start | bytes 1216512 | tf_op jit(solution)/shard_map/all_gather | solution.py:210
  97.3 298.5 %all-gather.54.cloned.1.call-start = ((), (), s32[]{:S(2)}) async-start(), calls=%async_computation.16 | async-start | bytes 3649536 | tf_op jit(solution)/shard_map/all_gather | solution.py:208
  98.1 353.6 %all-gather.56.cloned.1.call-start = ((), (), s32[]{:S(2)}) async-start(), calls=%async_computation.17 | async-start | bytes 1216512 | tf_op jit(solution)/shard_map/all_gather | solution.py:210
  98.8 380.2 %all-gather.42.cloned.1.call-start = ((), (), s32[]{:S(2)}) async-start(), calls=%async_computation.6 | async-start | bytes 2359296 | tf_op jit(solution)/shard_map/all_gather | solution.py:284
  99.1 113.0 %copy-start.66 = (f32[3072]{0:T(1024)}, f32[3072]{0:T(1024)S(1)}, u32[]{:S(2)}) copy-start(f32[3072]{0:T(1024)S(1)} %convert_element_type.304) | copy-start | bytes 36868
  99.2 113.0 %copy-start.52 = (f32[768]{0:T(1024)}, f32[768]{0:T(1024)S(1)}, u32[]{:S(2)}) copy-start(f32[768]{0:T(1024)S(1)} %convert_element_type.303) | copy-start | bytes 9220
  99.2 113.0 %copy-start.50 = (f32[768]{0:T(1024)}, f32[768]{0:T(1024)S(1)}, u32[]{:S(2)}) copy-start(f32[768]{0:T(1024)S(1)} %convert_element_type.302) | copy-start | bytes 9220
  336.6 65.6 %copy-start.16 = (f32[512,768]{1,0:T(8,128)}, f32[512,768]{1,0:T(8,128)S(1)}, u32[]{:S(2)}) copy-start(f32[512,768]{1,0:T(8,128)S(1)} %get-tuple-element.1185) | copy-start | bytes 4718596
  410.8 96.9 %all-gather.44.cloned.1.call-start = ((), (), s32[]{:S(2)}) async-start(), calls=%async_computation.7 | async-start | bytes 2359296 | tf_op jit(solution)/shard_map/all_gather | solution.py:283
  415.3 212.1 %all-gather.58.cloned.1.call-start = ((), (), s32[]{:S(2)}) async-start(), calls=%async_computation.18 | async-start | bytes 4866048 | tf_op jit(solution)/shard_map/all_gather | solution.py:212
  416.1 231.4 %all-gather.60.cloned.1.call-start = ((), (), s32[]{:S(2)}) async-start(), calls=%async_computation.19 | async-start | bytes 4866048 | tf_op jit(solution)/shard_map/all_gather | solution.py:214
  416.6 251.2 %reduce-scatter.5.cloned.1.call-start = ((), (), s32[]{:S(2)}) async-start(), calls=%async_computation.8 | async-start | bytes 2359296 | tf_op jit(solution)/shard_map/reduce_scatter | solution.py:396
  624.0 72.1 %reduce-scatter.7.cloned.1.call-start = ((), (), s32[]{:S(2)}) async-start(), calls=%async_computation.9 | async-start | bytes 2359296 | tf_op jit(solution)/shard_map/reduce_scatter | solution.py:399
  624.1 76.4 %copy-start.88 = (f32[768]{0:T(1024)}, f32[768]{0:T(1024)S(1)}, u32[]{:S(2)}) copy-start(f32[768]{0:T(1024)S(1)} %convert_element_type.310) | copy-start | bytes 9220
  627.4 384.4 %reduce-scatter.9.cloned.1.call-start = ((), (), s32[]{:S(2)}) async-start(), calls=%async_computation.10 | async-start | bytes 2359296 | tf_op jit(solution)/shard_map/reduce_scatter | solution.py:396
  773.3 242.1 %reduce-scatter.11.cloned.1.call-start = ((), (), s32[]{:S(2)}) async-start(), calls=%async_computation.11 | async-start | bytes 2359296 | tf_op jit(solution)/shard_map/reduce_scatter | solution.py:399
  971.4 1008.9 %all-reduce.22.cloned.1.call-start = ((), (), s32[]{:S(2)}) async-start(), calls=%async_computation.20 | async-start | bytes 113410048
  (106 other events, 1293.7 us)
Sparse Core Ops, SparseCore 0:
  11.5 62.9 all-gather.45
  89.8 25.4 all-gather.37
  117.4 27.2 all-gather.39
  148.0 64.1 all-gather.49
  215.5 62.4 all-gather.51
  280.8 52.9 all-gather.47
  336.7 59.0 all-gather.53
  398.7 52.9 all-gather.55
  453.3 25.6 all-gather.41
  480.4 27.1 all-gather.43
  511.1 64.0 all-gather.57
  578.6 62.4 all-gather.59
  643.3 24.4 reduce-scatter.4
  670.0 26.0 reduce-scatter.6
  773.4 26.0 reduce-scatter.8
  971.5 26.0 reduce-scatter.10
  1171.6 808.5 all-reduce.21
where the time goes:
time: 2020 us; the launch traced here: 2010 us
  waiting for transfers between devices  1130 us (56%)
  local copies, waits for them, and re-layouts  455 us (23%)
  matrix products  294 us (15%)
  other arithmetic  66.4 us (3%)
  blocking collectives  47 us (2%)
    unnamed x18, waiting for transfers between devices  801 us
    unnamed x265, local copies, waits for them, and re-layouts  226 us
    all_gather x2, waiting for transfers between devices, fetch_forward(): lax.all_gather(dense_weight[layer_index], ('seq', 'cp'), axis=0, tiled=True)  83.6 us
    reshape x2, local copies, waits for them, and re-layouts, per_device(): flat_terms = owner_rows(local_grads, owners).reshape(-1)  76.4 us
    all_gather x2, waiting for transfers between devices, fetch_forward(): lax.all_gather(qkv_weight[layer_index], ('seq', 'cp'), axis=0, tiled=True)  65.1 us
    reshape x22, local copies, waits for them, and re-layouts, owner_rows(): member.reshape(owners, -1)  51.5 us
    dot_general x8, matrix products, masked_scores(): jnp.einsum('qhd,khd->hqk', queries, block_keys, preferred_element_type=jn...  49.4 us
    all_gather x2, waiting for transfers between devices, layer_forward(): lax.all_gather(local_keys, 'cp', axis=0, tiled=True)  46.7 us
  transfers between devices with their start and end apart: 17, of which 13 were waited for; matrix products, arithmetic and copies ran while one was open for 26% of the time, Pallas kernels for 0%

commit v1 on v0

v1 whole, which is shorter than its diff:
```python
import functools

import jax
import jax.numpy as jnp
from jax import lax
from jax.experimental import pallas as pl
from jax.experimental.pallas import tpu as pltpu
from jax.sharding import PartitionSpec as P

HEADS = 12
HEAD_DIM = 64
ROT_DIM = 16
LAYERS = 2
LANES = 128
Q_BLOCK = 256

EPSILON = 1e-05
MASKED = -1e30
F32 = jnp.float32
BF16 = jnp.bfloat16
VMEM_LIMIT = 48 * 1024 * 1024


def pick(array, index, axis=0):
    return lax.dynamic_index_in_dim(array, index, axis, keepdims=False)


def dot_nn(left, right):
    return lax.dot_general(left, right, (((1,), (0,)), ((), ())), preferred_element_type=F32)


def dot_nt(left, right):
    return lax.dot_general(left, right, (((1,), (1,)), ((), ())), preferred_element_type=F32)


def dot_tn(left, right):
    return lax.dot_general(left, right, (((0,), (0,)), ((), ())), preferred_element_type=F32)


def cp_peer(array):
    return lax.ppermute(array, "cp", [(0, 1), (1, 0)])


def cp_gather(array):
    if lax.axis_size("cp") != 2:
        return lax.all_gather(array, "cp", axis=0, tiled=True)
    other = cp_peer(array)
    first = lax.axis_index("cp") == 0
    return jnp.concatenate([jnp.where(first, array, other), jnp.where(first, other, array)])


def cp_exchange(blocks):
    if lax.axis_size("cp") != 2:
        return lax.all_to_all(blocks, "cp", 0, 0)
    me = lax.axis_index("cp")
    mine = pick(blocks, me)
    other = cp_peer(pick(blocks, 1 - me).astype(BF16)).astype(blocks.dtype)
    first = me == 0
    return jnp.stack([jnp.where(first, mine, other), jnp.where(first, other, mine)])


def cp_sum(partial, low):
    if lax.axis_size("cp") != 2:
        return lax.psum(partial, "cp")
    return partial + cp_peer(low).astype(F32)


def cp_sends(partial, low, own_rows):
    if lax.axis_size("cp") != 2:
        if own_rows:
            return [(partial, lambda a: lax.psum_scatter(a, "cp", scatter_dimension=0, tiled=True))]
        return [(partial, lambda a: lax.psum(a, "cp"))]
    if own_rows:
        rows = partial.shape[0] // 2
        other = (1 - lax.axis_index("cp")) * rows
        low = lax.dynamic_slice_in_dim(low, other, rows, 0)
    return [(low, cp_peer)]


def cp_total(partial, brought, own_rows):
    if lax.axis_size("cp") != 2:
        return brought[0]
    if own_rows:
        rows = partial.shape[0] // 2
        partial = lax.dynamic_slice_in_dim(partial, lax.axis_index("cp") * rows, rows, 0)
    return partial + brought[0].astype(F32)


def cp_sum_rows(partial, low):
    if lax.axis_size("cp") != 2:
        return lax.psum_scatter(partial, "cp", scatter_dimension=0, tiled=True)
    rows = partial.shape[0] // 2
    me = lax.axis_index("cp")
    other = cp_peer(lax.dynamic_slice_in_dim(low, (1 - me) * rows, rows, 0))
    return lax.dynamic_slice_in_dim(partial, me * rows, rows, 0) + other.astype(F32)


def seq_shift(array, target):
    count = lax.axis_size("seq")
    return lax.ppermute(array, "seq", [(i, target(i) % count) for i in range(count)])


def ring_next(array):
    return seq_shift(array, lambda i: i + 4)


def pair_swap(array):
    return seq_shift(array, lambda i: i ^ 2)


def core_swap(array):
    return seq_shift(array, lambda i: i ^ 1)


def sum_everywhere(array):
    count = lax.axis_size("seq")
    if lax.axis_size("cp") != 2 or count & (count - 1):
        return lax.psum(array, ("seq", "cp"))
    array = array + cp_peer(array)
    bit = 1
    while bit < count:
        array = array + seq_shift(array, lambda i, bit=bit: i ^ bit)
        bit *= 2
    return array


def seq_place():
    me = lax.axis_index("seq")
    return me // 4, (me // 2) % 2, me % 2


def seq_gather(block, later):
    count = lax.axis_size("seq")
    if count % 8:
        return lax.all_gather(block, "seq", axis=0, tiled=True), later
    rings = count // 4
    ring, pair, core = seq_place()
    result = jnp.zeros((rings, 2, 2) + block.shape, block.dtype)
    held, waiting = block, []
    for step in range(rings):
        following = ring_next(held) if step < rings - 1 else None
        other = pair_swap(held)
        waiting.append(
            jnp.where(pair == 0, jnp.stack([held, other]), jnp.stack([other, held]))
        )
        held = following
        if step == rings - 2:
            held, later = lax.optimization_barrier((held, later))
        if step % 2 == 0:
            continue
        both = jnp.stack(waiting)
        sibling = core_swap(both)
        quads = jnp.where(
            core == 0, jnp.stack([both, sibling], axis=2), jnp.stack([sibling, both], axis=2)
        )
        for index in range(2):
            result = lax.dynamic_update_slice(
                result,
                quads[index : index + 1],
                ((ring - step + 1 - index) % rings,) + (0,) * (quads.ndim - 1),
            )
        waiting = []
    return result.reshape((count * block.shape[0],) + block.shape[1:]), later


def turn(block, cosine, sine_up, sine_down):
    return (
        block * cosine
        + pltpu.roll(block, LANES - ROT_DIM // 2, 1) * sine_up
        + pltpu.roll(block, ROT_DIM // 2, 1) * sine_down
    )


def turn_back(block, cosine, sine_up, sine_down):
    return (
        block * cosine
        + pltpu.roll(block * sine_up, ROT_DIM // 2, 1)
        + pltpu.roll(block * sine_down, LANES - ROT_DIM // 2, 1)
    )


def head_lanes(shape, head):
    lane = lax.broadcasted_iota(jnp.int32, shape, 1)
    return (lane < HEAD_DIM) if head == 0 else (lane >= HEAD_DIM)


def keys_first(rows):
    key_place = lax.broadcasted_iota(jnp.int32, (rows, rows), 0)
    query_place = lax.broadcasted_iota(jnp.int32, (rows, rows), 1)
    return key_place <= query_place


def forward_kernel(
    q_ref, k_ref, v_ref, query_pen, key_pen, out_ref, stat_ref, turned_t,
):
    rows = q_ref.shape[0]
    queries, keys, values = q_ref[...], k_ref[...], v_ref[...]
    value_t = values.astype(F32).T.astype(BF16)
    block = min(Q_BLOCK, rows)
    causal = keys_first(block)
    for head in range(2):
        lanes = head_lanes((rows, LANES), head)
        head_q = jnp.where(lanes, queries, query_pen[...])
        head_k = jnp.where(lanes, keys, key_pen[...])
        head_v = value_t[head * HEAD_DIM : (head + 1) * HEAD_DIM, :]
        for start in range(0, rows, block):
            stop = start + block
            scores = dot_nt(head_k[:stop], head_q[start:stop])
            last = jnp.where(causal, scores[start:], MASKED)
            scores = last if start == 0 else jnp.concatenate([scores[:start], last])
            top = jnp.max(scores, axis=0, keepdims=True)
            terms = jnp.exp(scores - top)
            total = jnp.sum(terms, axis=0, keepdims=True)
            summed = dot_nn(head_v[:, :stop], terms.astype(BF16))
            turned_t[head * HEAD_DIM : (head + 1) * HEAD_DIM, start:stop] = summed / total
            stat_ref[0, head : head + 1, start:stop] = top + jnp.log(total)
    out_ref[...] = turned_t[...].T.astype(BF16)


def attention_forward(queries, keys, values, penalties):
    rows, width = queries.shape
    pairs = width // LANES
    whole = pl.BlockSpec((rows, LANES), lambda p: (0, 0))
    column = pl.BlockSpec((rows, LANES), lambda p: (0, p))
    return pl.pallas_call(
        forward_kernel,
        grid=(pairs,),
        in_specs=[column] * 3 + [whole] * 2,
        out_specs=[column, pl.BlockSpec((1, 2, rows), lambda p: (p, 0, 0))],
        out_shape=[
            jax.ShapeDtypeStruct((rows, width), BF16),
            jax.ShapeDtypeStruct((pairs, 2, rows), F32),
        ],
        scratch_shapes=[pltpu.VMEM((LANES, rows), F32)],
        compiler_params=pltpu.CompilerParams(vmem_limit_bytes=VMEM_LIMIT),
        cost_estimate=pl.CostEstimate(
            flops=pairs * rows * rows * LANES,
            bytes_accessed=rows * width,
            transcendentals=0,
        ),
        name="attention_forward",
    )(queries, keys, values, *penalties)


def backward_kernel(
    q_ref, k_ref, v_ref, out_ref, grad_ref, stat_ref, cos_ref, up_ref, down_ref, query_pen, key_pen,
    mixed_ref, delta_t, grad_q,
):
    rows = q_ref.shape[0]
    width = mixed_ref.shape[1] // 3
    pair = pl.program_id(0)
    queries, keys, values, grads = q_ref[...], k_ref[...], v_ref[...], grad_ref[...]
    products = (grads.astype(F32) * out_ref[...].astype(F32)).T
    for head in range(2):
        delta_t[head : head + 1, :] = jnp.sum(
            products[head * HEAD_DIM : (head + 1) * HEAD_DIM, :], axis=0, keepdims=True
        )
    tables = (cos_ref[...], up_ref[...], down_ref[...])
    grad_q[...] = jnp.zeros_like(grad_q)
    block = min(Q_BLOCK, rows)
    causal = keys_first(block)
    none = jnp.zeros((rows, LANES), BF16)
    heads = []
    for head in range(2):
        lanes = head_lanes((rows, LANES), head)
        heads.append(
            (
                jnp.where(lanes, queries, query_pen[...]),
                jnp.where(lanes, keys, key_pen[...]),
                jnp.where(lanes, queries, none),
                jnp.where(lanes, keys, none),
                jnp.where(lanes, values, none),
                jnp.where(lanes, grads, none),
            )
        )
    for start in range(0, rows, block):
        stop = start + block
        grad_k, grad_v = None, None
        for head, (score_q, score_k, head_q, head_k, head_v, head_g) in enumerate(heads):
            scores = dot_nt(score_k[start:stop], score_q[start:])
            first = jnp.where(causal, scores[:, :block], MASKED)
            scores = (
                first if stop == rows else jnp.concatenate([first, scores[:, block:]], axis=1)
            )
            weights = jnp.exp(scores - stat_ref[0, head : head + 1, start:])
            grad_p = dot_nt(head_v[start:stop], head_g[start:])
            grad_s = (weights * (grad_p - delta_t[head : head + 1, start:])).astype(BF16)
            more_v = dot_nn(weights.astype(BF16), head_g[start:])
            more_k = dot_nn(grad_s, head_q[start:])
            grad_v = more_v if grad_v is None else grad_v + more_v
            grad_k = more_k if grad_k is None else grad_k + more_k
            grad_q[start:, :] += dot_tn(grad_s, head_k[start:stop])
        block_tables = tuple(table[start:stop] for table in tables)
        mixed_ref[start:stop, pl.ds(pl.multiple_of(width + pair * LANES, LANES), LANES)] = (
            turn_back(grad_k, *block_tables).astype(BF16)
        )
        mixed_ref[start:stop, pl.ds(pl.multiple_of(2 * width + pair * LANES, LANES), LANES)] = (
            grad_v.astype(BF16)
        )
    mixed_ref[:, pl.ds(pl.multiple_of(pair * LANES, LANES), LANES)] = turn_back(
        grad_q[...] * HEAD_DIM**-0.5, *tables
    ).astype(BF16)


def attention_backward(queries, keys, values, attended, grad_attended, stats, tables, penalties):
    rows, width = queries.shape
    pairs = width // LANES
    whole = pl.BlockSpec((rows, LANES), lambda p: (0, 0))
    column = pl.BlockSpec((rows, LANES), lambda p: (0, p))
    stat = pl.BlockSpec((1, 2, rows), lambda p: (p, 0, 0))
    return pl.pallas_call(
        backward_kernel,
        grid=(pairs,),
        in_specs=[column] * 5 + [stat] + [whole] * 5,
        out_specs=pl.BlockSpec((rows, 3 * width), lambda p: (0, 0)),
        out_shape=jax.ShapeDtypeStruct((rows, 3 * width), BF16),
        scratch_shapes=[pltpu.VMEM((2, rows), F32), pltpu.VMEM((rows, LANES), F32)],
        compiler_params=pltpu.CompilerParams(vmem_limit_bytes=VMEM_LIMIT),
        cost_estimate=pl.CostEstimate(
            flops=pairs * rows * rows * LANES,
            bytes_accessed=rows * width,
            transcendentals=0,
        ),
        name="attention_backward",
    )(queries, keys, values, attended, grad_attended, stats, *tables, *penalties)


ROW_BLOCK = 256


def layer_norm(hidden):
    average = jnp.mean(hidden, axis=-1, keepdims=True)
    centered = hidden - average
    variance = jnp.mean(centered * centered, axis=-1, keepdims=True)
    inverse_std = lax.rsqrt(variance + EPSILON)
    return centered * inverse_std, inverse_std


def load_parts(parts, semaphores):
    copies = [
        pltpu.make_async_copy(source, target, semaphores.at[index])
        for index, (source, target) in enumerate(parts)
    ]
    first = pl.program_id(0) == 0

    @pl.when(first)
    def _():
        for copy in copies:
            copy.start()

    def wait(*indices):
        @pl.when(first)
        def _():
            for index in indices:
                copies[index].wait()

    return wait


def down_parts(source, sizes, target):
    if sizes.slabs == 0:
        return [(source, target)]
    first, rows, features = sizes.split + sizes.hidden, sizes.rows, sizes.features
    parts = []
    for group in range(sizes.groups):
        for slab in range(sizes.slabs):
            lanes = slice(first + slab * features, first + (slab + 1) * features)
            start = (group * sizes.slabs + slab) * rows
            parts.append(
                (
                    source.at[group * rows : (group + 1) * rows, lanes],
                    target.at[start : start + rows, :],
                )
            )
    return parts


def project_kernel(
    sizes, hidden, gain, bias, qkv_bias, whole, cos_ref, up_ref, down_ref,
    attn_in, q_ref, k_ref, v_ref, qkv, semaphores,
):
    width = sizes.width
    wait = load_parts([(whole.at[:, : 3 * width], qkv)], semaphores)
    normed, _ = layer_norm(hidden[...])
    low = (normed * gain[...] + bias[...]).astype(BF16)
    attn_in[...] = low
    wait(0)
    tables = (cos_ref[...], up_ref[...], down_ref[...])
    mixed = dot_nn(low, qkv[...]) + qkv_bias[...]
    for start in range(0, width, LANES):
        lanes = slice(start, start + LANES)
        turned = turn(mixed[:, start : start + LANES], *tables).astype(BF16)
        q_ref[:, lanes] = turned * jnp.asarray(HEAD_DIM**-0.5, BF16)
        first = width + start
        k_ref[:, lanes] = turn(mixed[:, first : first + LANES], *tables).astype(BF16)
    v_ref[...] = mixed[:, 2 * width :].astype(BF16)


def row_call(kernel, sizes, rows, operands, results, scratch, copies, flops, name):
    block = min(ROW_BLOCK, rows)

    def spec(shape, kind):
        if kind == "hbm":
            return pl.BlockSpec(memory_space=pl.ANY)
        if kind == "rows":
            return pl.BlockSpec((block, shape[1]), lambda i: (i, 0))
        return pl.BlockSpec(shape, lambda i: (0, 0))

    return pl.pallas_call(
        functools.partial(kernel, sizes),
        grid=(rows // block,),
        in_specs=[spec(array.shape, kind) for array, kind in operands],
        out_specs=[spec(shape, kind) for shape, _, kind in results],
        out_shape=[jax.ShapeDtypeStruct(shape, dtype) for shape, dtype, _ in results],
        scratch_shapes=scratch + [pltpu.SemaphoreType.DMA((copies,))],
        compiler_params=pltpu.CompilerParams(vmem_limit_bytes=VMEM_LIMIT),
        cost_estimate=pl.CostEstimate(
            flops=flops // 8, bytes_accessed=rows * sizes.features, transcendentals=0
        ),
        name=name,
    )(*[array for array, _ in operands])


def project(hidden, weights, tables, sizes):
    rows, features, width = hidden.shape[0], sizes.features, sizes.width
    return row_call(
        project_kernel, sizes, rows,
        [(hidden, "rows"), (weights["gain_attn"], "all"), (weights["bias_attn"], "all"),
         (weights["qkv_bias"], "all"), (weights["whole"], "hbm")]
        + [(table, "rows") for table in tables],
        [((rows, features), BF16, "rows")] + [((rows, width), BF16, "rows")] * 3,
        [pltpu.VMEM((features, 3 * width), BF16)], 1,
        2 * rows * features * 3 * width, "project",
    )


ERFC_TERMS = (
    0.17087277, -0.82215223, 1.48851587, -1.13520398, 0.27886807,
    -0.18628806, 0.09678418, 0.37409196, 1.00002368, -1.26551223,
)


def gelu_and_slope(upper):
    size = jnp.abs(upper) * 0.5**0.5
    inverse = 1.0 / (1.0 + 0.5 * size)
    series = inverse * ERFC_TERMS[0] + ERFC_TERMS[1]
    for term in ERFC_TERMS[2:]:
        series = series * inverse + term
    square = size * size
    tail = 0.5 * inverse * jnp.exp(series - square)
    below = jnp.where(upper < 0, tail, 1.0 - tail)
    slope = below + upper * (jnp.exp(-square) * 0.3989422804014327)
    return upper * below, slope


def branches_kernel(
    sizes, hidden, attended, gain, bias, up_bias, whole, down_source, dense,
    mlp_in, activated, slope_ref, partial, partial_low, up, down, upper, semaphores,
):
    up_part = (whole.at[:, sizes.split : sizes.split + sizes.hidden], up)
    downs = down_parts(down_source, sizes, down)
    wait = load_parts([up_part] + downs, semaphores)
    normed, _ = layer_norm(hidden[...])
    low = (normed * gain[...] + bias[...]).astype(BF16)
    mlp_in[...] = low
    total = dot_nn(attended[...], dense[...])
    wait(0)
    upper[...] = dot_nn(low, up[...]) + up_bias[...]
    units = upper.shape[1]
    tile = 512 if units % 512 == 0 else LANES

    @pl.loop(0, upper.shape[0], step=16)
    def _(first):
        rows = pl.ds(pl.multiple_of(first, 16), 16)
        for start in range(0, units, tile):
            lanes = slice(start, start + tile)
            act, slope = gelu_and_slope(upper[rows, lanes])
            activated[rows, lanes] = act.astype(BF16)
            slope_ref[rows, lanes] = slope.astype(BF16)

    wait(*range(1, 1 + len(downs)))
    total = total + dot_nn(activated[...], down[...])
    partial[...] = total
    partial_low[...] = total.astype(BF16)


def branches(hidden, attended, weights, sizes):
    rows, features, units, width = hidden.shape[0], sizes.features, sizes.hidden, sizes.width
    return row_call(
        branches_kernel, sizes, rows,
        [(hidden, "rows"), (attended, "rows"), (weights["gain_mlp"], "all"),
         (weights["bias_mlp"], "all"), (weights["up_bias"], "all"), (weights["whole"], "hbm"),
         (weights["down"], "hbm"), (weights["dense"], "all")],
        [((rows, features), BF16, "rows")] + [((rows, units), BF16, "rows")] * 2
        + [((rows, features), F32, "rows"), ((rows, features), BF16, "rows")],
        [pltpu.VMEM((features, units), BF16), pltpu.VMEM((units, features), BF16),
         pltpu.VMEM((min(ROW_BLOCK, rows), units), F32)],
        1 + sizes.down_copies, 2 * rows * features * (2 * units + width), "branches",
    )


def add_sums(ref, index, block):
    ref[index : index + 1, :] += jnp.sum(block, axis=0, keepdims=True)


def branches_back_kernel(
    sizes, low_ref, slope, hidden, gain, whole, down_source, dense,
    grad_attended, grad_upper, grad_mlp, sums, unit_sums, up, down, semaphores,
):
    downs = down_parts(down_source, sizes, down)
    up_part = (whole.at[:, sizes.split : sizes.split + sizes.hidden], up)
    wait = load_parts(downs + [up_part], semaphores)

    @pl.when(pl.program_id(0) == 0)
    def _():
        sums[...] = jnp.zeros_like(sums)
        unit_sums[...] = jnp.zeros_like(unit_sums)

    low = low_ref[...]
    grad_attended[...] = dot_nt(low, dense[...]).astype(BF16)
    normed, _ = layer_norm(hidden[...])
    wait(*range(len(downs)))
    upper = (dot_nt(low, down[...]) * slope[...].astype(F32)).astype(BF16)
    grad_upper[...] = upper
    add_sums(unit_sums, 0, upper.astype(F32))
    wait(len(downs))
    grad = dot_nt(upper, up[...])
    add_sums(sums, 0, grad * normed)
    add_sums(sums, 1, grad)
    add_sums(sums, 2, low.astype(F32))
    grad_mlp[...] = grad * gain[...]


def branches_back(low, slope, hidden, weights, sizes):
    rows, features, units, width = hidden.shape[0], sizes.features, sizes.hidden, sizes.width
    return row_call(
        branches_back_kernel, sizes, rows,
        [(low, "rows"), (slope, "rows"), (hidden, "rows"), (weights["gain_mlp"], "all"),
         (weights["whole"], "hbm"), (weights["down"], "hbm"), (weights["dense"], "all")],
        [((rows, width), BF16, "rows"), ((rows, units), BF16, "rows"),
         ((rows, features), F32, "rows"), ((8, features), F32, "all"), ((8, units), F32, "all")],
        [pltpu.VMEM((features, units), BF16), pltpu.VMEM((units, features), BF16)],
        1 + sizes.down_copies, 2 * rows * features * (2 * units + width), "branches_back",
    )


def project_back_kernel(
    sizes, mixed, grad_mlp, hidden, gain, whole, partial, partial_low, sums, mixed_sums, qkv,
    semaphores,
):
    wait = load_parts([(whole.at[:, : 3 * sizes.width], qkv)], semaphores)

    @pl.when(pl.program_id(0) == 0)
    def _():
        sums[...] = jnp.zeros_like(sums)
        mixed_sums[...] = jnp.zeros_like(mixed_sums)

    normed, inverse_std = layer_norm(hidden[...])
    add_sums(mixed_sums, 0, mixed[...].astype(F32))
    wait(0)
    grad = dot_nt(mixed[...], qkv[...])
    add_sums(sums, 0, grad * normed)
    add_sums(sums, 1, grad)
    grad = grad * gain[...] + grad_mlp[...]
    centered = (
        grad
        - jnp.mean(grad, axis=-1, keepdims=True)
        - normed * jnp.mean(grad * normed, axis=-1, keepdims=True)
    )
    grad = inverse_std * centered
    partial[...] = grad
    partial_low[...] = grad.astype(BF16)


def project_back(grad_mixed, grad_mlp, hidden, weights, sizes):
    rows, features, width = hidden.shape[0], sizes.features, sizes.width
    return row_call(
        project_back_kernel, sizes, rows,
        [(grad_mixed, "rows"), (grad_mlp, "rows"), (hidden, "rows"),
         (weights["gain_attn"], "all"), (weights["whole"], "hbm")],
        [((rows, features), F32, "rows"), ((rows, features), BF16, "rows"),
         ((8, features), F32, "all"), ((8, 3 * width), F32, "all")],
        [pltpu.VMEM((features, 3 * width), BF16)], 1,
        2 * rows * features * 3 * width, "project_back",
    )


def lay_out(refs, widths, sizes, store):
    first = 0
    for ref, width in zip(refs, widths):
        if width is None:
            for slab in range(sizes.slabs):
                rows = slice(slab * sizes.rows, (slab + 1) * sizes.rows)
                store(ref[rows, :], slice(first, first + sizes.features))
                first += sizes.features
        else:
            store(ref[...], slice(first, first + width))
            first += width


def pack_kernel(sizes, widths, place, *refs):
    packed = refs[-1]

    def store(block, lanes):
        packed[0, 0, :, lanes] = block

    lay_out(refs[:-1], widths, sizes, store)


def first_sum_kernel(sizes, widths, place, *refs):
    count = len(widths)
    sibling_sent, sibling_mine, sent, mine = refs[2 * count :]

    def store_sent(block, lanes):
        total = block.astype(F32) + sibling_sent[0, 0, :, lanes].astype(F32)
        sent[0, :, lanes] = total.astype(BF16)

    def store_mine(block, lanes):
        mine[0, :, lanes] = block.astype(F32) + sibling_mine[0, 0, :, lanes].astype(F32)

    lay_out(refs[:count], widths, sizes, store_sent)
    lay_out(refs[count : 2 * count], widths, sizes, store_mine)


class Scatter:
    def __init__(self, parts, sizes):
        self.sizes, self.stage, self.operands, self.result = sizes, 0, [], None
        self.rings = sizes.groups // 4
        self.kernels = sizes.groups % 8 == 0 and sizes.rows % 16 == 0
        self.parts = [
            part if owned else (part if part.shape[0] == sizes.features else sizes.pack_down(part))
            for part, owned in ((part, self.kernels) for part in parts)
        ]
        self.widths = [
            part.shape[1] if part.shape[0] == sizes.features else None for part in self.parts
        ]
        self.columns = sum(part.size for part in self.parts) // sizes.features
        if not self.kernels:
            packed = jnp.concatenate(self.parts, axis=1)
            summed = lax.psum_scatter(packed, "seq", scatter_dimension=0, tiled=True)
            self.result = summed.astype(F32)
            return
        ring, pair, core = seq_place()
        self.place = jnp.stack([ring, pair, core]).astype(jnp.int32)
        self.operands = [self.pack()]

    def cost(self):
        return pl.CostEstimate(
            flops=0, bytes_accessed=self.sizes.features * self.columns * 4, transcendentals=0
        )

    def specs(self, index):
        rows = self.sizes.rows
        return [
            pl.BlockSpec((rows * (self.sizes.slabs if width is None else 1), part.shape[1]), index)
            for part, width in zip(self.parts, self.widths)
        ]

    def pack(self):
        def other(ring, pair, place):
            return ((ring * 2 + pair) * 2 + 1 - place[2], 0)

        rows, rings = self.sizes.rows, self.rings
        return pl.pallas_call(
            functools.partial(pack_kernel, self.sizes, self.widths),
            grid_spec=pltpu.PrefetchScalarGridSpec(
                num_scalar_prefetch=1,
                grid=(rings, 2),
                in_specs=self.specs(other),
                out_specs=pl.BlockSpec((1, 1, rows, self.columns), lambda r, p, place: (r, p, 0, 0)),
            ),
            out_shape=jax.ShapeDtypeStruct((rings, 2, rows, self.columns), BF16),
            compiler_params=pltpu.CompilerParams(vmem_limit_bytes=VMEM_LIMIT),
            cost_estimate=self.cost(),
            name="pack_terms",
        )(self.place, *self.parts)

    def first_sum(self):
        rows, rings, columns = self.sizes.rows, self.rings, self.columns

        def ring_of(step, place):
            return lax.rem(place[0] + 2 * rings - 1 - step, rings)

        def own(pair_of):
            return lambda step, place: (
                (ring_of(step, place) * 2 + pair_of(place)) * 2 + place[2],
                0,
            )

        def sibling(pair_of):
            return pl.BlockSpec(
                (1, 1, rows, columns),
                lambda step, place: (ring_of(step, place), pair_of(place), 0, 0),
            )

        def away(place):
            return 1 - place[1]

        def home(place):
            return place[1]

        step_block = pl.BlockSpec((1, rows, columns), lambda step, place: (step, 0, 0))
        return pl.pallas_call(
            functools.partial(first_sum_kernel, self.sizes, self.widths),
            grid_spec=pltpu.PrefetchScalarGridSpec(
                num_scalar_prefetch=1,
                grid=(rings,),
                in_specs=self.specs(own(away))
                + self.specs(own(home))
                + [sibling(away), sibling(home)],
                out_specs=[step_block, step_block],
            ),
            out_shape=[
                jax.ShapeDtypeStruct((rings, rows, columns), BF16),
                jax.ShapeDtypeStruct((rings, rows, columns), F32),
            ],
            compiler_params=pltpu.CompilerParams(vmem_limit_bytes=VMEM_LIMIT),
            cost_estimate=self.cost(),
            name="first_sum",
        )(self.place, *self.parts, *self.parts, self.sibling, self.sibling)

    def launch(self, operands):
        if self.stage == 0:
            return [core_swap(operands[0])]
        if self.stage == 1:
            self.arrived = [pair_swap(operand) for operand in operands]
            return self.arrived[:1]
        return [ring_next(operands[0])]

    def land(self, received):
        if self.stage == 0:
            self.sibling = received[0]
        elif self.stage == 1:
            self.arrived[0] = received[0]
        else:
            self.received = received[0]
        self.stage += 1

    def prepare(self):
        if self.result is not None or self.stage == 0:
            return
        half = self.rings // 2
        if self.stage == 1:
            sent, self.mine = self.first_sum()
            self.operands = [sent[:half], sent[half:]]
            return
        step = self.stage - 2
        total = self.mine[step] + self.arrived[step // half][step % half].astype(F32)
        if step > 0:
            total = total + self.received.astype(F32)
        if step == self.rings - 1:
            self.result, self.operands = total, []
        else:
            self.operands = [total.astype(BF16)]


def beside(scatters, inputs, compute, sends=()):
    scatters = [scatter for scatter in scatters if scatter.result is None]
    for scatter in scatters:
        scatter.prepare()
    scatters = [scatter for scatter in scatters if scatter.result is None]
    operands = [scatter.operands for scatter in scatters]
    inputs, operands, sent = lax.optimization_barrier(
        (tuple(inputs), operands, [operand for operand, _ in sends])
    )
    landing = [scatter.launch(operand) for scatter, operand in zip(scatters, operands)]
    brought = [transfer(operand) for operand, (_, transfer) in zip(sent, sends)]
    short = [scatter.stage == 0 for scatter in scatters]
    tied = [received for received, is_short in zip(landing, short) if is_short]
    results, tied, brought = lax.optimization_barrier((compute(*inputs), tied, brought))
    for scatter, received, is_short in zip(scatters, landing, short):
        scatter.land(tied.pop(0) if is_short else received)
    return results, brought


def finish(scatters):
    while any(scatter.result is None for scatter in scatters):
        for scatter in scatters:
            if scatter.result is None:
                scatter.prepare()
            if scatter.result is None:
                scatter.land(scatter.launch(scatter.operands))


def rotary_tables(positions):
    half_rot = ROT_DIM // 2
    inverse = 10000.0 ** (-(jnp.arange(half_rot, dtype=F32) * 2.0 / ROT_DIM))
    angles = positions.astype(F32)[:, None] * inverse[None, :]
    cosine, sine = jnp.cos(angles), jnp.sin(angles)
    rows = positions.shape[0]
    rest = HEAD_DIM - ROT_DIM
    zeros = jnp.zeros_like(sine)
    still = jnp.zeros((rows, rest), F32)
    cosine = jnp.concatenate([cosine, cosine, jnp.ones((rows, rest), F32)] * 2, axis=1)
    sine_up = jnp.concatenate([-sine, zeros, still] * 2, axis=1)
    sine_down = jnp.concatenate([zeros, sine, still] * 2, axis=1)
    return cosine, sine_up, sine_down


def document_penalties(docs):
    slots = jnp.arange(LANES, dtype=jnp.int32) % HEAD_DIM
    same = docs[:, None] == slots[None, :]
    return jnp.where(same, 0.0, MASKED).astype(BF16), same.astype(BF16)


def pad_heads(array, axis, sizes):
    missing = sizes.members * sizes.width - HEADS * HEAD_DIM
    if missing == 0:
        return array
    pads = [(0, 0)] * array.ndim
    pads[axis] = (0, missing)
    return jnp.pad(array, pads)


class Sizes:
    def __init__(self, features, hidden):
        self.members, self.groups = lax.axis_size("cp"), lax.axis_size("seq")
        per_member = -(-HEADS // self.members)
        self.padded = self.members * (per_member + per_member % 2)
        self.width = self.padded // self.members * HEAD_DIM
        self.features = features
        self.rows = features // self.groups
        owned = hidden // (self.members * self.groups)
        self.slabs = owned // self.rows if owned % self.rows == 0 and self.rows % 16 == 0 else 0
        self.down_copies = max(self.slabs * self.groups, 1)
        self.hidden = hidden // self.members
        self.ratio = hidden // features
        self.split = 3 * self.width + features
        self.owned = features // (self.members * self.groups)

    def pack_down(self, rows):
        if self.slabs == 0:
            return rows.reshape(-1, self.hidden)
        rows = rows.reshape(-1, self.slabs, self.rows, self.features)
        return jnp.transpose(rows, (0, 2, 1, 3)).reshape(-1, self.hidden)

    def unpack_down(self, packed):
        if self.slabs == 0:
            return packed.reshape(-1, self.features)
        packed = packed.reshape(-1, self.rows, self.slabs, self.features)
        return jnp.transpose(packed, (0, 2, 1, 3)).reshape(-1, self.features)


def to_users(rows, sizes, back=False):
    count = sizes.members * sizes.groups
    moves = [(i, (i % sizes.groups) * sizes.members + i // sizes.groups) for i in range(count)]
    if back:
        moves = [(target, source) for source, target in moves]
    return lax.ppermute(rows, ("seq", "cp"), moves)


def cut_columns(params, sizes):
    qkv_weight, dense_weight, up_weight = params[4], params[6], params[8]
    layers, rows, members = qkv_weight.shape[0], qkv_weight.shape[1], sizes.members
    qkv = pad_heads(qkv_weight.reshape(layers, rows, 3, HEADS * HEAD_DIM), 3, sizes)
    shares = []
    for member in range(members):
        heads = slice(member * sizes.width, (member + 1) * sizes.width)
        units = slice(member * sizes.hidden, (member + 1) * sizes.hidden)
        shares.append(
            jnp.concatenate(
                [qkv[:, :, part, heads] for part in range(3)]
                + [dense_weight, up_weight[:, :, units]],
                axis=2,
            )
        )
    return jnp.stack(shares)


def fetch_layers(params, exchanged, down, sizes, tokens):
    packed = [
        jnp.concatenate(
            [
                exchanged[:, layer].reshape(-1, exchanged.shape[-1]),
                sizes.pack_down(down[layer]),
            ],
            axis=1,
        )
        for layer in range(LAYERS)
    ]
    first, later = seq_gather(packed[0], packed[1:] + [tokens])
    fetched = [unpack_layer(first, sizes)]
    for block in later[:-1]:
        whole = lax.all_gather(block, "seq", axis=0, tiled=True)
        fetched.append(unpack_layer(whole, sizes))
    return fetched, later[-1]


def fetch_vectors(params, sizes):
    vectors = [params[i] for i in (0, 1, 2, 3, 7, 11, 5, 9)]
    me = lax.axis_index("cp")
    owner = lax.axis_index("seq") * sizes.members + me
    layers = vectors[0].shape[0]
    placed = [
        lax.dynamic_update_slice(
            jnp.zeros((layers, vector.shape[1] * sizes.members * sizes.groups), BF16),
            vector,
            (0, owner * vector.shape[1]),
        )
        for vector in vectors
    ]
    widths = [vector.shape[1] for vector in placed]
    every = sum_everywhere(jnp.concatenate(placed, axis=1)).astype(F32)
    results = []
    for layer in range(layers):
        first, arrays = 0, []
        for width in widths:
            arrays.append(every[layer : layer + 1, first : first + width])
            first += width
        gain_attn, bias_attn, gain_mlp, bias_mlp, dense_bias, down_bias, qkv_bias, up_bias = arrays
        qkv_bias = pad_heads(qkv_bias.reshape(3, HEADS * HEAD_DIM), 1, sizes)
        qkv_bias = lax.dynamic_slice_in_dim(qkv_bias, me * sizes.width, sizes.width, 1)
        up_bias = lax.dynamic_slice_in_dim(up_bias, me * sizes.hidden, sizes.hidden, 1)
        results.append(
            {
                "qkv_bias": qkv_bias.reshape(1, -1), "up_bias": up_bias,
                "gain_attn": gain_attn, "bias_attn": bias_attn,
                "gain_mlp": gain_mlp, "bias_mlp": bias_mlp,
                "out_bias": dense_bias + down_bias,
            }
        )
    return results


def unpack_layer(whole, sizes):
    split, features = sizes.split, sizes.features
    dense = whole[:, 3 * sizes.width : split]
    down = whole if sizes.slabs else sizes.unpack_down(whole[:, split + sizes.hidden :])
    dense = jnp.pad(dense, ((0, sizes.members * sizes.width - features), (0, 0)))
    dense = lax.dynamic_slice_in_dim(
        dense, lax.axis_index("cp") * sizes.width, sizes.width, 0
    )
    return {"whole": whole, "dense": dense, "down": down}


def layer_forward(hidden, weights, tables, penalties, sizes):
    attn_in, queries, keys, values = project(hidden, weights, tables, sizes)
    attended, stats = attention_forward(queries, keys, values, penalties)
    mlp_in, activated, slope, partial, partial_low = branches(hidden, attended, weights, sizes)
    kept = (hidden, attn_in, mlp_in, queries, keys, values, stats, attended, activated, slope)
    return partial, partial_low, kept


def layer_backward(low, weights, kept, tables, penalties, sizes, earlier, later_sum):
    last = earlier is not None
    hidden, attn_in, mlp_in, queries, keys, values, stats, attended, activated, slope = kept
    grad_attended, grad_upper, grad_mlp, mlp_sums, unit_sums = branches_back(
        low, slope, hidden, weights, sizes
    )
    terms = branch_terms(low, activated, mlp_in, grad_upper, attended, sizes)
    terms, grad_attended = lax.optimization_barrier((terms, grad_attended))
    if last:
        scatters = [Scatter(terms + earlier, sizes)]
        summed = later_sum
    else:
        scatters = []
        packed = jnp.concatenate([terms[0], sizes.pack_down(terms[1]), terms[2]], axis=1)
        packed, grad_attended = lax.optimization_barrier((packed, grad_attended))
        summed = lax.psum_scatter(packed, "seq", scatter_dimension=0, tiled=True)
    (grad_mixed,), _ = beside(
        scatters,
        (grad_attended,),
        lambda grads: (
            attention_backward(
                queries, keys, values, attended, grads, stats, tables, penalties
            ),
        ),
    )
    if last:
        later_sum, grad_mixed = lax.optimization_barrier((later_sum, grad_mixed))
    (partial, partial_low, attn_sums, mixed_sums), _ = beside(
        scatters,
        (grad_mixed,),
        lambda mixed: project_back(mixed, grad_mlp, hidden, weights, sizes),
    )
    grad_qkv, brought = beside(
        [],
        (grad_mixed,),
        lambda mixed: dot_tn(attn_in, mixed).astype(BF16),
        cp_sends(partial, partial_low, last),
    )
    sums = vector_sums(attn_sums, mlp_sums, mixed_sums, unit_sums, sizes)
    if last:
        summed = later_sum
        scatters.append(Scatter([grad_qkv], sizes))
    return cp_total(partial, brought, last), sums, summed, grad_qkv, scatters


def branch_terms(low, activated, mlp_in, grad_upper, attended, sizes):
    up = dot_tn(mlp_in, grad_upper).astype(BF16)
    down = dot_tn(activated, low).astype(BF16)
    dense = jnp.zeros((sizes.members * sizes.width, sizes.features), BF16)
    dense = lax.dynamic_update_slice_in_dim(
        dense, dot_tn(attended, low).astype(BF16), lax.axis_index("cp") * sizes.width, 0
    )
    return [up, down, dense[: sizes.features]]


def vector_sums(attn_sums, mlp_sums, qkv_bias, up_bias, sizes):
    me = lax.axis_index("cp")
    local, padded = sizes.width, sizes.members * sizes.width
    out_bias = jnp.where(me == 0, mlp_sums[2:3], 0.0)
    rows = [attn_sums[0:1], attn_sums[1:2], mlp_sums[0:1], mlp_sums[1:2], out_bias]
    for part in range(3):
        row = jnp.zeros((1, padded), F32)
        row = lax.dynamic_update_slice(
            row, qkv_bias[0:1, part * local : (part + 1) * local], (0, me * local)
        )
        rows.append(row[:, : HEADS * HEAD_DIM])
    up = jnp.zeros((1, sizes.members * sizes.hidden), F32)
    rows.append(lax.dynamic_update_slice(up, up_bias[0:1], (0, me * sizes.hidden)))
    return jnp.concatenate(rows, axis=1)


def finish_gradients(summed, sizes):
    members, features, hidden, width = sizes.members, sizes.features, sizes.hidden, sizes.width
    rows = summed.shape[0] // members
    down = sizes.unpack_down(summed[:, hidden : 2 * hidden]).astype(BF16)
    down = to_users(down, sizes, back=True).astype(F32)
    joined = jnp.concatenate([summed[:, :hidden], summed[:, 2 * hidden :]], axis=1)
    joined = cp_exchange(joined.reshape(members, rows, -1))
    up = jnp.transpose(joined[:, :, :hidden], (1, 0, 2)).reshape(rows, -1)
    dense = jnp.sum(joined[:, :, hidden : hidden + features], axis=0)
    qkv = joined[:, :, hidden + features :].reshape(members, rows, 3, width)
    qkv = jnp.transpose(qkv, (1, 2, 0, 3)).reshape(rows, 3, members * width)
    qkv = qkv[:, :, : HEADS * HEAD_DIM].reshape(rows, -1)
    return qkv, dense, up, down


def per_device(inputs, doc_ids, cotangent, *params):
    sizes = Sizes(inputs.shape[1], params[8].shape[2])
    small = (0, 1, 2, 3, 5, 7, 9, 11)
    docs = cp_gather(doc_ids)
    exchanged, docs, inputs, cotangent, vectors = lax.optimization_barrier(
        (
            cp_exchange(cut_columns(params, sizes)), docs, inputs, cotangent,
            [params[index] for index in small],
        )
    )
    params = list(params)
    for index, vector in zip(small, vectors):
        params[index] = vector
    tokens = jnp.stack([inputs, cotangent])
    if sizes.members == 2:
        fetched, other = fetch_layers(
            params, exchanged, to_users(params[10], sizes), sizes, cp_peer(tokens)
        )
        first = lax.axis_index("cp") == 0
        both = jnp.stack([jnp.where(first, tokens, other), jnp.where(first, other, tokens)])
    else:
        fetched, tokens = fetch_layers(
            params, exchanged, to_users(params[10], sizes), sizes, tokens
        )
        both = cp_gather(tokens[None])
    vectors = fetch_vectors(params, sizes)
    for layer in range(LAYERS):
        fetched[layer].update(vectors[layer])
    both = both.astype(F32)
    hidden = both[:, 0].reshape(-1, inputs.shape[1])
    low = both[:, 1].reshape(-1, inputs.shape[1]).astype(BF16)
    place = jnp.arange(docs.shape[0], dtype=jnp.int32)
    starts = jnp.sum((docs[None, :] < docs[:, None]).astype(jnp.int32), axis=1)
    tables = rotary_tables(place - starts)
    penalties = document_penalties(docs)
    me = lax.axis_index("cp")
    rows = inputs.shape[0]

    def own_rows(array):
        return lax.dynamic_slice_in_dim(array, me * rows, rows, 0)

    records = []
    for layer in range(LAYERS):
        partial, partial_low, kept = layer_forward(
            hidden, fetched[layer], tables, penalties, sizes
        )
        records.append(kept)
        out_bias = fetched[layer]["out_bias"]
        if layer < LAYERS - 1:
            hidden = hidden + cp_sum(partial, partial_low) + out_bias
        else:
            output = own_rows(hidden) + cp_sum_rows(partial, partial_low) + out_bias
    vector_terms, summed, earlier, layer_sum = [], [], None, None
    upstream = low.astype(F32)
    for layer in reversed(range(LAYERS)):
        total, sums, layer_sum, grad_qkv, scatters = layer_backward(
            low, fetched[layer], records[layer], tables, penalties, sizes, earlier, layer_sum
        )
        vector_terms.append(sums)
        if layer == 0:
            summed[-1:] = [layer_sum]
        else:
            summed.append(layer_sum)
        if layer > 0:
            earlier = (earlier or []) + [grad_qkv]
            upstream = upstream + total
            low = upstream.astype(BF16)
        else:
            input_grad = own_rows(upstream) + total
    flat = sum_everywhere(jnp.concatenate(vector_terms[::-1]))
    finish(scatters)
    mixed, last_qkv = scatters[0].result, scatters[1].result
    first = 2 * sizes.hidden + sizes.features
    width = 3 * sizes.width
    sums = [jnp.concatenate([mixed[:, :first], last_qkv], axis=1)] + [
        jnp.concatenate(
            [
                summed[index].astype(F32),
                mixed[:, first + index * width : first + (index + 1) * width],
            ],
            axis=1,
        )
        for index in range(LAYERS - 1)
    ][::-1]
    qkv, dense, up, down = (
        jnp.stack(grads) for grads in zip(*(finish_gradients(part, sizes) for part in sums))
    )
    owner, features = lax.axis_index("seq") * sizes.members + me, sizes.features
    own, first = [], 0
    for blocks in (1, 1, 1, 1, 1, 3, sizes.ratio):
        share = blocks * sizes.owned
        own.append(lax.dynamic_slice_in_dim(flat, first + owner * share, share, 1))
        first += blocks * features
    gain_attn, bias_attn, gain_mlp, bias_mlp, out_bias, qkv_bias, up_bias = own
    return (
        output.astype(BF16), input_grad, gain_attn, bias_attn, gain_mlp, bias_mlp, qkv, qkv_bias,
        dense, out_bias, up, up_bias, down, out_bias,
    )


def solution(mesh):
    rows, shared = P(("seq", "cp")), P(None, ("seq", "cp"))
    return jax.shard_map(
        per_device,
        mesh=mesh,
        in_specs=(rows,) * 3 + (shared,) * 12,
        out_specs=(rows,) * 2 + (shared,) * 12,
        check_vma=False,
    )
```

time: 2020 us -> 569 us (0.28)
  waiting for transfers between devices: 1130 us -> 196 us
  local copies, waits for them, and re-layouts: 455 us -> 43.3 us
  matrix products: 294 us -> 22.8 us
  Pallas kernels: 0 us -> 175 us
  starting transfers between devices: 0.9 us -> 63 us
  blocking collectives: 47 us -> 0 us
  other arithmetic: 66.4 us -> 44 us
    unnamed x18 -> x2, waiting for transfers between devices: 801 us -> 0.03 us
    all_gather x12 -> x1, waiting for transfers between devices: 294 us -> 0.01 us  [fetch_layers(): whole = lax.all_gather(block, 'seq', axis=0, tiled=True)]
    dot_general x52 -> x8, matrix products: 294 us -> 22.8 us  [dot_tn(): lax.dot_general(left, right, (((0,), (0,)), ((), ())), preferred_element_...]
    unnamed x265 -> x169, local copies, waits for them, and re-layouts: 226 us -> 20 us
    ppermute x0 -> x43, waiting for transfers between devices: none -> 195 us  [the longest x29 108 us: seq_shift(): lax.ppermute(array, 'seq', [(i, target(i) % count) for i in range(count)])]
    pallas_call x0 -> x16, Pallas kernels: none -> 175 us  [the longest x8 108 us: row_call(): pl.pallas_call(functools.partial(kernel, sizes), grid=(rows // block,), i...]
    reshape x24 -> x6, local copies, waits for them, and re-layouts: 128 us -> 3.42 us  [the longest x1 2.19 us: pack_down(): rows = rows.reshape(-1, self.slabs, self.rows, self.features)]
    ppermute x0 -> x43, starting transfers between devices: none -> 62.7 us  [the longest x29 40.8 us: seq_shift(): lax.ppermute(array, 'seq', [(i, target(i) % count) for i in range(count)])]
  transfers between devices with their start and end apart: 17 -> 45, of which waited for: 13 -> 21; matrix products, arithmetic and copies ran while one was open for 26% -> 12% of each run, Pallas kernels for 0% -> 20%
where the time goes in v1:
time: 569 us; the launch traced here: 560 us
  waiting for transfers between devices  196 us (34%)
  Pallas kernels  175 us (31%)
  starting transfers between devices  63 us (11%)
  other arithmetic  44 us (8%)
  local copies, waits for them, and re-layouts  43.3 us (8%)
  matrix products  22.8 us (4%)
  between operations  16.5 us (3%)
    ppermute x29, waiting for transfers between devices, seq_shift(): lax.ppermute(array, 'seq', [(i, target(i) % count) for i in range(count)])  108 us
    pallas_call x8, Pallas kernels, row_call(): pl.pallas_call(functools.partial(kernel, sizes), grid=(rows // block,), i...  108 us
    ppermute x11, waiting for transfers between devices, cp_peer(): return lax.ppermute(array, 'cp', [(0, 1), (1, 0)])  83 us
    ppermute x29, starting transfers between devices, seq_shift(): lax.ppermute(array, 'seq', [(i, target(i) % count) for i in range(count)])  40.8 us
    pallas_call x2, Pallas kernels, attention_backward(): pl.pallas_call(backward_kernel, grid=(pairs,), in_specs=[column] * 5 + [s...  29.6 us
    pallas_call x2, Pallas kernels, attention_forward(): pl.pallas_call(forward_kernel, grid=(pairs,), in_specs=[column] * 3 + [wh...  23.2 us
    dot_general x8, matrix products, dot_tn(): lax.dot_general(left, right, (((0,), (0,)), ((), ())), preferred_element_...  22.8 us
    unnamed x169, local copies, waits for them, and re-layouts  20 us
  transfers between devices with their start and end apart: 45, of which 21 were waited for; matrix products, arithmetic and copies ran while one was open for 12% of the time, Pallas kernels for 20%

profile of v1, /device:TPU:1, one launch (start us, length us, event | category | flops | bytes accessed | tf_op | source)
XLA Modules:
  0.0 560.3 jit_solution(8372684375828889664)
XLA Ops:
  15.2 13.0 %collective-permute-done.1 = s32[512]{0:T(512)S(1)} collective-permute-done((s32[512]{0:T(512)S(1)}, s32[512]{0:T(512)S(1)}, u32[]{:S(2)}, u32[]{:S(2)}) %collective-permute-start.1) | collective-permute-done | bytes 2080 | tf_op jit(solution)/shard_map/ppermute | solution.py:41
  56.4 12.1 %collective-permute-done.4 = bf16[48,4992]{1,0:T(8,128)(2,1)S(1)} collective-permute-done((bf16[48,4992]{1,0:T(8,128)(2,1)}, bf16[48,4992]{1,0:T(8,128)(2,1)S(1)}, u32[]{:S(2)}, u32[]{:S(2)}) %collective-permute-start.4) | collective-permute-done | bytes 479264 | tf_op jit(solution)/shard_map/ppermute | solution.py:100
  69.4 10.5 %collective-permute-done.5 = bf16[48,4992]{1,0:T(8,128)(2,1)S(1)} collective-permute-done((bf16[48,4992]{1,0:T(8,128)(2,1)S(1)}, bf16[48,4992]{1,0:T(8,128)(2,1)S(1)}, u32[]{:S(2)}, u32[]{:S(2)}) %collective-permute-start.5) | collective-permute-done | bytes 479264 | tf_op jit(solution)/shard_map/ppermute | solution.py:100
  90.8 14.4 %collective-permute-start.14 = (bf16[2,2,48,4992]{3,2,1,0:T(8,128)(2,1)S(1)}, bf16[2,2,48,4992]{3,2,1,0:T(8,128)(2,1)S(1)}, u32[]{:S(2)}, u32[]{:S(2)}) collective-permute-start(bf16[2,2,48,4992]{3,2,1,0:T(8,128)(2,1)S(1)} %get-tuple-element.203), channel_id=1, source_target_pairs={{0,2},{2,0},{4,6},{6,4},{8,10},{10,8},{12,14},{14,12},{16,18},{18,... | collective-permute-start | bytes 5750792 | tf_op jit(solution)/shard_map/ppermute | solution.py:100
  115.0 6.3 %collective-permute-start.17 = (bf16[2,2,48,4992]{3,2,1,0:T(8,128)(2,1)S(1)}, bf16[2,2,48,4992]{3,2,1,0:T(8,128)(2,1)S(1)}, u32[]{:S(2)}, u32[]{:S(2)}) collective-permute-start(bf16[2,2,48,4992]{3,2,1,0:T(8,128)(2,1)S(1)} %get-tuple-element.201), channel_id=1, source_target_pairs={{0,2},{2,0},{4,6},{6,4},{8,10},{10,8},{12,14},{14,12},{16,18},{18,... | collective-permute-start | bytes 5750792 | tf_op jit(solution)/shard_map/ppermute | solution.py:100
  129.6 7.0 %project.2 = (bf16[1024,768]{1,0:T(8,128)(2,1)S(1)}, bf16[1024,384]{1,0:T(8,128)(2,1)S(1)}, bf16[1024,384]{1,0:T(8,128)(2,1)S(1)}, bf16[1024,384]{1,0:T(8,128)(2,1)S(1)}) custom-call(f32[1024,768]{1,0:T(8,128)} %bitcast_convert_fusion.hidden, f32[1,768]{1,0:T(1,128)S(1)} %get-tuple-element.237.gain, f32[1,768]{1,0:T(1,128)S(1)} %get-tuple-element.236.bias, ...), custom_call_target="tpu_custom_call" | custom-call | flops 226492416 | bytes 786432 | tf_op jit(solution)/shard_map/project/pallas_call | solution.py:409
  137.7 11.4 %attention_forward.2 = (bf16[1024,384]{1,0:T(8,128)(2,1)S(1)}, f32[3,2,1024]{2,1,0:T(2,128)S(1)}) custom-call(bf16[1024,384]{1,0:T(8,128)(2,1)S(1)} %get-tuple-element.114.q_ref, bf16[1024,384]{1,0:T(8,128)(2,1)S(1)} %get-tuple-element.115.k_ref, bf16[1024,384]{1,0:T(8,128)(2,1)S(1)} %get-tuple-element.116.v_ref, bf16[1024,128]{1,0:T(8,128)(2,1)S(1)} %fusion.7.query_pen, ...), custom_call_target="tpu_custom_call" | custom-call | flops 402653184 | bytes 393216 | tf_op jit(solution)/shard_map/attention_forward/pallas_call | solution.py:225
  149.3 23.9 %branches.2 = (bf16[1024,768]{1,0:T(8,128)(2,1)S(1)}, bf16[1024,1536]{1,0:T(8,128)(2,1)}, bf16[1024,1536]{1,0:T(8,128)(2,1)}, f32[1024,768]{1,0:T(8,128)}, bf16[1024,768]{1,0:T(8,128)(2,1)}) custom-call(f32[1024,768]{1,0:T(8,128)} %bitcast_convert_fusion.hidden, bf16[1024,384]{1,0:T(8,128)(2,1)S(1)} %get-tuple-element.117.attended.out_ref, ...), custom_call_target="tpu_custom_call" | custom-call | flops 679477248 | bytes 786432 | tf_op jit(solution)/shard_map/branches/pallas_call | solution.py:409
  175.3 34.9 %collective-permute-done.18 = bf16[1024,768]{1,0:T(8,128)(2,1)} collective-permute-done((bf16[1024,768]{1,0:T(8,128)(2,1)}, bf16[1024,768]{1,0:T(8,128)(2,1)}, u32[]{:S(2)}, u32[]{:S(2)}) %collective-permute-start.18) | collective-permute-done | bytes 1572896 | tf_op jit(solution)/shard_map/ppermute | solution.py:41
  216.6 7.0 %project.3 = (bf16[1024,768]{1,0:T(8,128)(2,1)S(1)}, bf16[1024,384]{1,0:T(8,128)(2,1)S(1)}, bf16[1024,384]{1,0:T(8,128)(2,1)S(1)}, bf16[1024,384]{1,0:T(8,128)(2,1)S(1)}) custom-call(f32[1024,768]{1,0:T(8,128)} %add_add_fusion.1.hidden, f32[1,768]{1,0:T(1,128)S(1)} %get-tuple-element.231.gain, f32[1,768]{1,0:T(1,128)S(1)} %get-tuple-element.230.bias, ...), custom_call_target="tpu_custom_call" | custom-call | flops 226492416 | bytes 786432 | tf_op jit(solution)/shard_map/project/pallas_call | solution.py:409
  224.8 11.8 %attention_forward.3 = (bf16[1024,384]{1,0:T(8,128)(2,1)S(1)}, f32[3,2,1024]{2,1,0:T(2,128)S(1)}) custom-call(bf16[1024,384]{1,0:T(8,128)(2,1)S(1)} %get-tuple-element.121.q_ref, bf16[1024,384]{1,0:T(8,128)(2,1)S(1)} %get-tuple-element.122.k_ref, bf16[1024,384]{1,0:T(8,128)(2,1)S(1)} %get-tuple-element.123.v_ref, bf16[1024,128]{1,0:T(8,128)(2,1)S(1)} %fusion.7.query_pen, ...), custom_call_target="tpu_custom_call" | custom-call | flops 402653184 | bytes 393216 | tf_op jit(solution)/shard_map/attention_forward/pallas_call | solution.py:225
  236.6 23.6 %branches.3 = (bf16[1024,768]{1,0:T(8,128)(2,1)S(1)}, bf16[1024,1536]{1,0:T(8,128)(2,1)}, bf16[1024,1536]{1,0:T(8,128)(2,1)}, f32[1024,768]{1,0:T(8,128)}, bf16[1024,768]{1,0:T(8,128)(2,1)S(1)}) custom-call(f32[1024,768]{1,0:T(8,128)} %add_add_fusion.1.hidden, bf16[1024,384]{1,0:T(8,128)(2,1)S(1)} %get-tuple-element.124.attended.out_ref, ...), custom_call_target="tpu_custom_call" | custom-call | flops 679477248 | bytes 786432 | tf_op jit(solution)/shard_map/branches/pallas_call | solution.py:409
  266.3 13.8 %branches_back.2 = (bf16[1024,384]{1,0:T(8,128)(2,1)S(1)}, bf16[1024,1536]{1,0:T(8,128)(2,1)S(1)}, f32[1024,768]{1,0:T(8,128)}, f32[8,768]{1,0:T(8,128)S(1)}, f32[8,1536]{1,0:T(8,128)S(1)}) custom-call(bf16[1024,768]{1,0:T(8,128)(2,1)S(1)} %bitcast.163, bf16[1024,1536]{1,0:T(8,128)(2,1)} %get-tuple-element.128.slope, f32[1024,768]{1,0:T(8,128)} %add_add_fusion.1.hidden, ...), custom_call_target="tpu_custom_call" | custom-call | flops 679477248 | bytes 786432 | tf_op jit(solution)/shard_map/branches_back/pallas_call | solution.py:409
  295.5 14.7 %attention_backward.2.mixed = bf16[1024,1152]{1,0:T(8,128)(2,1)} custom-call(bf16[1024,384]{1,0:T(8,128)(2,1)S(1)} %copy-done.20, bf16[1024,384]{1,0:T(8,128)(2,1)S(1)} %copy-done.22, bf16[1024,384]{1,0:T(8,128)(2,1)S(1)} %copy-done.24, bf16[1024,384]{1,0:T(8,128)(2,1)S(1)} %copy-done.6, bf16[1024,384]{1,0:T(8,128)(2,1)S(1)} %copy-done.26, ...), custom_call_target="tpu_custom_call" | custom-call | flops 402653184 | bytes 393216 | tf_op jit(solution)/shard_map/attention_backward/pallas_call | solution.py:311
  311.9 9.4 %project_back.2 = (f32[1024,768]{1,0:T(8,128)}, bf16[1024,768]{1,0:T(8,128)(2,1)S(1)}, f32[8,768]{1,0:T(8,128)S(1)}, f32[8,1152]{1,0:T(8,128)S(1)}) custom-call(bf16[1024,1152]{1,0:T(8,128)(2,1)S(1)} %copy-done.2, f32[1024,768]{1,0:T(8,128)} %get-tuple-element.138.grad_mlp, f32[1024,768]{1,0:T(8,128)} %add_add_fusion.1.hidden, ...), custom_call_target="tpu_custom_call" | custom-call | flops 226492416 | bytes 786432 | tf_op jit(solution)/shard_map/project_back/pallas_call | solution.py:409
  324.6 31.0 %collective-permute-done.20 = bf16[1024,768]{1,0:T(8,128)(2,1)S(1)} collective-permute-done((bf16[1024,768]{1,0:T(8,128)(2,1)S(1)}, bf16[1024,768]{1,0:T(8,128)(2,1)S(1)}, u32[]{:S(2)}, u32[]{:S(2)}) %collective-permute-start.20) | collective-permute-done | bytes 1572896 | tf_op jit(solution)/shard_map/ppermute | solution.py:41
  358.0 13.9 %branches_back.3 = (bf16[1024,384]{1,0:T(8,128)(2,1)S(1)}, bf16[1024,1536]{1,0:T(8,128)(2,1)S(1)}, f32[1024,768]{1,0:T(8,128)}, f32[8,768]{1,0:T(8,128)S(1)}, f32[8,1536]{1,0:T(8,128)S(1)}) custom-call(bf16[1024,768]{1,0:T(8,128)(2,1)S(1)} %get-tuple-element.190.low_ref, bf16[1024,1536]{1,0:T(8,128)(2,1)} %get-tuple-element.147.slope, ...), custom_call_target="tpu_custom_call" | custom-call | flops 679477248 | bytes 786432 | tf_op jit(solution)/shard_map/branches_back/pallas_call | solution.py:409
  380.7 7.4 %pack_terms.2 = bf16[4,2,48,4992]{3,2,1,0:T(8,128)(2,1)} custom-call(s32[3]{0:T(128)S(1)} %pad_add_fusion.1.place, bf16[768,1536]{1,0:T(8,128)(2,1)S(1)} %convolution_convert_fusion.1.refs_0_.refs_4_, bf16[1536,768]{1,0:T(8,128)(2,1)} %convolution_convert_fusion.refs_1_.refs_5_, bf16[768,768]{1,0:T(8,128)(2,1)S(1)} %fusion.1.refs_2_.refs_6_, ...), custom_call_target="tpu_custom_call" | custom-call | bytes 15335424 | tf_op jit(solution)/shard_map/pack_terms/pallas_call | solution.py:664
  390.9 14.9 %attention_backward.3.mixed = bf16[1024,1152]{1,0:T(8,128)(2,1)} custom-call(bf16[1024,384]{1,0:T(8,128)(2,1)S(1)} %copy-done.14, bf16[1024,384]{1,0:T(8,128)(2,1)S(1)} %copy-done.16, bf16[1024,384]{1,0:T(8,128)(2,1)S(1)} %copy-done.18, bf16[1024,384]{1,0:T(8,128)(2,1)S(1)} %copy-done.4, bf16[1024,384]{1,0:T(8,128)(2,1)S(1)} %get-tuple-element.156.grad_ref, ...), custom_call_target="tpu_custom_call" | custom-call | flops 402653184 | bytes 393216 | tf_op jit(solution)/shard_map/attention_backward/pallas_call | solution.py:311
  414.1 9.1 %project_back.3 = (f32[1024,768]{1,0:T(8,128)}, bf16[1024,768]{1,0:T(8,128)(2,1)S(1)}, f32[8,768]{1,0:T(8,128)S(1)}, f32[8,1152]{1,0:T(8,128)S(1)}) custom-call(bf16[1024,1152]{1,0:T(8,128)(2,1)S(1)} %copy-done.1, f32[1024,768]{1,0:T(8,128)} %get-tuple-element.164.grad_mlp, f32[1024,768]{1,0:T(8,128)} %bitcast_convert_fusion.hidden, ...), custom_call_target="tpu_custom_call" | custom-call | flops 226492416 | bytes 786432 | tf_op jit(solution)/shard_map/project_back/pallas_call | solution.py:409
  435.4 21.9 %collective-permute-done.25 = f32[2,9216]{1,0:T(2,128)S(1)} collective-permute-done((f32[2,9216]{1,0:T(2,128)S(1)}, f32[2,9216]{1,0:T(2,128)S(1)}, u32[]{:S(2)}, u32[]{:S(2)}) %collective-permute-start.25) | collective-permute-done | bytes 73760 | tf_op jit(solution)/shard_map/ppermute | solution.py:100
  485.0 12.5 %collective-permute-done.30 = bf16[48,4992]{1,0:T(8,128)(2,1)S(1)} collective-permute-done((bf16[48,4992]{1,0:T(8,128)(2,1)S(1)}, bf16[48,4992]{1,0:T(8,128)(2,1)S(1)}, u32[]{:S(2)}, u32[]{:S(2)}) %collective-permute-start.30) | collective-permute-done | bytes 479264 | tf_op jit(solution)/shard_map/ppermute | solution.py:100
  499.6 15.1 %collective-permute-done.36 = bf16[48,1152]{1,0:T(8,128)(2,1)S(1)} collective-permute-done((bf16[48,1152]{1,0:T(8,128)(2,1)S(1)}, bf16[48,1152]{1,0:T(8,128)(2,1)S(1)}, u32[]{:S(2)}, u32[]{:S(2)}) %collective-permute-start.36) | collective-permute-done | bytes 110624 | tf_op jit(solution)/shard_map/ppermute | solution.py:100
  523.3 9.1 %collective-permute-done.38 = bf16[48,1152]{1,0:T(8,128)(2,1)S(1)} collective-permute-done((bf16[48,1152]{1,0:T(8,128)(2,1)S(1)}, bf16[48,1152]{1,0:T(8,128)(2,1)S(1)}, u32[]{:S(2)}, u32[]{:S(2)}) %collective-permute-start.38) | collective-permute-done | bytes 110624 | tf_op jit(solution)/shard_map/ppermute | solution.py:100
  (428 shorter events, 195.2 us)
Async XLA Ops:
  7.2 208.0 %all-gather.2.cloned.1.call-start = ((), (), s32[]{:S(2)}) async-start(), calls=%async_computation.1 | async-start | bytes 8146944 | tf_op jit(solution)/shard_map/all_gather | solution.py:884
  7.2 21.0 %collective-permute-start.2 = (bf16[2,96,768]{2,1,0:T(8,128)(2,1)}, bf16[2,96,768]{2,1,0:T(8,128)(2,1)S(1)}, u32[]{:S(2)}, u32[]{:S(2)}) collective-permute-start(bf16[2,96,768]{2,1,0:T(8,128)(2,1)} %param.28), channel_id=1, source_target_pairs={{0,0},{1,2},{2,4},{3,6},{4,8},{5,10},{6,12},{7,14},{8,16},{9,18},{... | collective-permute-start | bytes 884744 | tf_op jit(solution)/shard_map/ppermute | solution.py:849
  13.6 15.0 %collective-permute-start = (bf16[2,24,3456]{2,1,0:T(8,128)(2,1)S(1)}, bf16[2,24,3456]{2,1,0:T(8,128)(2,1)S(1)}, u32[]{:S(2)}, u32[]{:S(2)}) collective-permute-start(bf16[2,24,3456]{2,1,0:T(8,128)(2,1)S(1)} %fusion.14), channel_id=1, source_target_pairs={{0,1},{1,0},{2,3},{3,2},{4,5},{5,4},{6,7},{7,6},{8,9},{9,8},{10,11... | collective-permute-start | bytes 995336 | tf_op jit(solution)/shard_map/ppermute | solution.py:41
  30.1 26.0 %collective-permute-start.3 = (bf16[48,4992]{1,0:T(8,128)(2,1)}, bf16[48,4992]{1,0:T(8,128)(2,1)}, u32[]{:S(2)}, u32[]{:S(2)}) collective-permute-start(bf16[48,4992]{1,0:T(8,128)(2,1)} %get-tuple-element.213), channel_id=1, source_target_pairs={{0,8},{2,10},{4,12},{6,14},{8,16},{10,18},{12,20},{14,22},{16,24},... | collective-permute-start | bytes 1437704 | tf_op jit(solution)/shard_map/ppermute | solution.py:100
  30.1 50.2 %collective-permute-start.12 = (bf16[48,4992]{1,0:T(8,128)(2,1)}, bf16[48,4992]{1,0:T(8,128)(2,1)}, u32[]{:S(2)}, u32[]{:S(2)}) collective-permute-start(bf16[48,4992]{1,0:T(8,128)(2,1)} %get-tuple-element.213), channel_id=1, source_target_pairs={{0,4},{2,6},{4,0},{6,2},{8,12},{10,14},{12,8},{14,10},{16,20},{18,... | collective-permute-start | bytes 1437704 | tf_op jit(solution)/shard_map/ppermute | solution.py:100
  38.3 41.6 %collective-permute-start.6 = (bf16[2,512,768]{2,1,0:T(8,128)(2,1)}, bf16[2,512,768]{2,1,0:T(8,128)(2,1)}, u32[]{:S(2)}, u32[]{:S(2)}) collective-permute-start(bf16[2,512,768]{2,1,0:T(8,128)(2,1)} %pad_maximum_fusion.4), channel_id=1, source_target_pairs={{0,1},{1,0},{2,3},{3,2},{4,5},{5,4},{6,7},{7,6},{8,9},{9,8},{10,11... | collective-permute-start | bytes 4718600 | tf_op jit(solution)/shard_map/ppermute | solution.py:41
  79.9 333.2 %reduce-scatter.2.cloned.1.call-start = ((), (), s32[]{:S(2)}) async-start(), calls=%async_computation.2 | async-start | bytes 6266880 | tf_op jit(solution)/shard_map/reduce_scatter | solution.py:959
  82.1 23.1 %collective-permute-start.15 = (bf16[48,4992]{1,0:T(8,128)(2,1)S(1)}, bf16[48,4992]{1,0:T(8,128)(2,1)S(1)}, u32[]{:S(2)}, u32[]{:S(2)}) collective-permute-start(bf16[48,4992]{1,0:T(8,128)(2,1)S(1)} %copy-done.52), channel_id=1, source_target_pairs={{0,4},{2,6},{4,0},{6,2},{8,12},{10,14},{12,8},{14,10},{16,20},{18,... | collective-permute-start | bytes 1437704 | tf_op jit(solution)/shard_map/ppermute | solution.py:100
  90.8 30.6 %collective-permute-start.14 = (bf16[2,2,48,4992]{3,2,1,0:T(8,128)(2,1)S(1)}, bf16[2,2,48,4992]{3,2,1,0:T(8,128)(2,1)S(1)}, u32[]{:S(2)}, u32[]{:S(2)}) collective-permute-start(bf16[2,2,48,4992]{3,2,1,0:T(8,128)(2,1)S(1)} %get-tuple-element.203), channel_id=1, source_target_pairs={{0,2},{2,0},{4,6},{6,4},{8,10},{10,8},{12,14},{14,12},{16,18},{18,... | collective-permute-start | bytes 5750792 | tf_op jit(solution)/shard_map/ppermute | solution.py:100
  174.3 35.9 %collective-permute-start.18 = (bf16[1024,768]{1,0:T(8,128)(2,1)}, bf16[1024,768]{1,0:T(8,128)(2,1)}, u32[]{:S(2)}, u32[]{:S(2)}) collective-permute-start(bf16[1024,768]{1,0:T(8,128)(2,1)} %get-tuple-element.119), channel_id=1, source_target_pairs={{0,1},{1,0},{2,3},{3,2},{4,5},{5,4},{6,7},{7,6},{8,9},{9,8},{10,11... | collective-permute-start | bytes 4718600 | tf_op jit(solution)/shard_map/ppermute | solution.py:41
  321.3 34.4 %collective-permute-start.20 = (bf16[1024,768]{1,0:T(8,128)(2,1)S(1)}, bf16[1024,768]{1,0:T(8,128)(2,1)S(1)}, u32[]{:S(2)}, u32[]{:S(2)}) collective-permute-start(bf16[1024,768]{1,0:T(8,128)(2,1)S(1)} %get-tuple-element.143), channel_id=1, source_target_pairs={{0,1},{1,0},{2,3},{3,2},{4,5},{5,4},{6,7},{7,6},{8,9},{9,8},{10,11... | collective-permute-start | bytes 4718600 | tf_op jit(solution)/shard_map/ppermute | solution.py:41
  388.1 17.7 %collective-permute-start.21 = (bf16[4,2,48,4992]{3,2,1,0:T(8,128)(2,1)}, bf16[4,2,48,4992]{3,2,1,0:T(8,128)(2,1)}, u32[]{:S(2)}, u32[]{:S(2)}) collective-permute-start(bf16[4,2,48,4992]{3,2,1,0:T(8,128)(2,1)} %pack_terms.2), channel_id=1, source_target_pairs={{0,2},{2,0},{4,6},{6,4},{8,10},{10,8},{12,14},{14,12},{16,18},{18,... | collective-permute-start | bytes 11501576 | tf_op jit(solution)/shard_map/ppermute | solution.py:100
  430.7 26.6 %collective-permute-start.19 = (bf16[512,768]{1,0:T(8,128)(2,1)S(1)}, bf16[512,768]{1,0:T(8,128)(2,1)S(1)}, u32[]{:S(2)}, u32[]{:S(2)}) collective-permute-start(bf16[512,768]{1,0:T(8,128)(2,1)S(1)} %constant_dynamic-slice_fusion.8), channel_id=1, source_target_pairs={{0,1},{1,0},{2,3},{3,2},{4,5},{5,4},{6,7},{7,6},{8,9},{9,8},{10,11... | collective-permute-start | bytes 2359304 | tf_op jit(solution)/shard_map/ppermute | solution.py:41
  431.7 50.2 %collective-permute-start.29 = (bf16[2,48,4992]{2,1,0:T(8,128)(2,1)}, bf16[2,48,4992]{2,1,0:T(8,128)(2,1)}, u32[]{:S(2)}, u32[]{:S(2)}) collective-permute-start(bf16[2,48,4992]{2,1,0:T(8,128)(2,1)} %get-tuple-element.181), channel_id=1, source_target_pairs={{0,4},{2,6},{4,0},{6,2},{8,12},{10,14},{12,8},{14,10},{16,20},{18,... | collective-permute-start | bytes 2875400 | tf_op jit(solution)/shard_map/ppermute | solution.py:100
  434.1 23.2 %collective-permute-start.25 = (f32[2,9216]{1,0:T(2,128)S(1)}, f32[2,9216]{1,0:T(2,128)S(1)}, u32[]{:S(2)}, u32[]{:S(2)}) collective-permute-start(f32[2,9216]{1,0:T(2,128)S(1)} %fusion.64), channel_id=1, source_target_pairs={{0,4},{2,6},{4,0},{6,2},{8,12},{10,14},{12,8},{14,10},{16,20},{18,... | collective-permute-start | bytes 221192 | tf_op jit(solution)/shard_map/ppermute | solution.py:100
  435.1 45.1 %collective-permute-start.22 = (bf16[512,768]{1,0:T(8,128)(2,1)}, bf16[512,768]{1,0:T(8,128)(2,1)}, u32[]{:S(2)}, u32[]{:S(2)}) collective-permute-start(bf16[512,768]{1,0:T(8,128)(2,1)} %constant_dynamic-slice_fusion.7), channel_id=1, source_target_pairs={{0,1},{1,0},{2,3},{3,2},{4,5},{5,4},{6,7},{7,6},{8,9},{9,8},{10,11... | collective-permute-start | bytes 2359304 | tf_op jit(solution)/shard_map/ppermute | solution.py:41
  461.3 53.5 %collective-permute-start.28 = (bf16[2,48,4992]{2,1,0:T(8,128)(2,1)}, bf16[2,48,4992]{2,1,0:T(8,128)(2,1)}, u32[]{:S(2)}, u32[]{:S(2)}) collective-permute-start(bf16[2,48,4992]{2,1,0:T(8,128)(2,1)} %get-tuple-element.180), channel_id=1, source_target_pairs={{0,4},{2,6},{4,0},{6,2},{8,12},{10,14},{12,8},{14,10},{16,20},{18,... | collective-permute-start | bytes 2875400 | tf_op jit(solution)/shard_map/ppermute | solution.py:100
  463.1 77.8 %collective-permute-start.42 = (bf16[96,768]{1,0:T(8,128)(2,1)}, bf16[96,768]{1,0:T(8,128)(2,1)}, u32[]{:S(2)}, u32[]{:S(2)}) collective-permute-start(bf16[96,768]{1,0:T(8,128)(2,1)} %bitcast.66), channel_id=1, source_target_pairs={{0,0},{2,1},{4,2},{6,3},{8,4},{10,5},{12,6},{14,7},{16,8},{18,9},{... | collective-permute-start | bytes 442376 | tf_op jit(solution)/shard_map/ppermute | solution.py:849
  483.1 14.4 %collective-permute-start.30 = (bf16[48,4992]{1,0:T(8,128)(2,1)S(1)}, bf16[48,4992]{1,0:T(8,128)(2,1)S(1)}, u32[]{:S(2)}, u32[]{:S(2)}) collective-permute-start(bf16[48,4992]{1,0:T(8,128)(2,1)S(1)} %fusion.8), channel_id=1, source_target_pairs={{0,8},{2,10},{4,12},{6,14},{8,16},{10,18},{12,20},{14,22},{16,24},... | collective-permute-start | bytes 1437704 | tf_op jit(solution)/shard_map/ppermute | solution.py:100
  484.9 14.0 %collective-permute-start.35 = (bf16[2,48,1152]{2,1,0:T(8,128)(2,1)S(1)}, bf16[2,48,1152]{2,1,0:T(8,128)(2,1)S(1)}, u32[]{:S(2)}, u32[]{:S(2)}) collective-permute-start(bf16[2,48,1152]{2,1,0:T(8,128)(2,1)S(1)} %get-tuple-element.215), channel_id=1, source_target_pairs={{0,4},{2,6},{4,0},{6,2},{8,12},{10,14},{12,8},{14,10},{16,20},{18,... | collective-permute-start | bytes 663560 | tf_op jit(solution)/shard_map/ppermute | solution.py:100
  498.8 16.0 %collective-permute-start.31 = (bf16[48,4992]{1,0:T(8,128)(2,1)S(1)}, bf16[48,4992]{1,0:T(8,128)(2,1)S(1)}, u32[]{:S(2)}, u32[]{:S(2)}) collective-permute-start(bf16[48,4992]{1,0:T(8,128)(2,1)S(1)} %fusion.3), channel_id=1, source_target_pairs={{0,8},{2,10},{4,12},{6,14},{8,16},{10,18},{12,20},{14,22},{16,24},... | collective-permute-start | bytes 1437704 | tf_op jit(solution)/shard_map/ppermute | solution.py:100
  498.9 15.8 %collective-permute-start.36 = (bf16[48,1152]{1,0:T(8,128)(2,1)S(1)}, bf16[48,1152]{1,0:T(8,128)(2,1)S(1)}, u32[]{:S(2)}, u32[]{:S(2)}) collective-permute-start(bf16[48,1152]{1,0:T(8,128)(2,1)S(1)} %fusion.30), channel_id=1, source_target_pairs={{0,8},{2,10},{4,12},{6,14},{8,16},{10,18},{12,20},{14,22},{16,24},... | collective-permute-start | bytes 331784 | tf_op jit(solution)/shard_map/ppermute | solution.py:100
  499.6 16.4 %collective-permute-start.34 = (bf16[2,48,1152]{2,1,0:T(8,128)(2,1)S(1)}, bf16[2,48,1152]{2,1,0:T(8,128)(2,1)S(1)}, u32[]{:S(2)}, u32[]{:S(2)}) collective-permute-start(bf16[2,48,1152]{2,1,0:T(8,128)(2,1)S(1)} %get-tuple-element.214), channel_id=1, source_target_pairs={{0,4},{2,6},{4,0},{6,2},{8,12},{10,14},{12,8},{14,10},{16,20},{18,... | collective-permute-start | bytes 663560 | tf_op jit(solution)/shard_map/ppermute | solution.py:100
  516.0 16.4 %collective-permute-start.32 = (bf16[48,4992]{1,0:T(8,128)(2,1)S(1)}, bf16[48,4992]{1,0:T(8,128)(2,1)S(1)}, u32[]{:S(2)}, u32[]{:S(2)}) collective-permute-start(bf16[48,4992]{1,0:T(8,128)(2,1)S(1)} %fusion.4), channel_id=1, source_target_pairs={{0,8},{2,10},{4,12},{6,14},{8,16},{10,18},{12,20},{14,22},{16,24},... | collective-permute-start | bytes 1437704 | tf_op jit(solution)/shard_map/ppermute | solution.py:100
  (90 other events, 844.8 us)
Sparse Core Ops, SparseCore 0:
  80.1 74.5 all-gather.1
  288.9 81.4 reduce-scatter.1

commit v2 on v1

--- a/solution.py
+++ b/solution.py
@@ -455,7 +455,7 @@
 
 def branches_kernel(
     sizes, hidden, attended, gain, bias, up_bias, whole, down_source, dense,
-    mlp_in, activated, slope_ref, partial, partial_low, up, down, upper, semaphores,
+    mlp_in, activated, slope_ref, partial, partial_low, up, down, semaphores,
 ):
     up_part = (whole.at[:, sizes.split : sizes.split + sizes.hidden], up)
     downs = down_parts(down_source, sizes, down)
@@ -465,21 +465,12 @@
     mlp_in[...] = low
     total = dot_nn(attended[...], dense[...])
     wait(0)
-    upper[...] = dot_nn(low, up[...]) + up_bias[...]
-    units = upper.shape[1]
-    tile = 512 if units % 512 == 0 else LANES
-
-    @pl.loop(0, upper.shape[0], step=16)
-    def _(first):
-        rows = pl.ds(pl.multiple_of(first, 16), 16)
-        for start in range(0, units, tile):
-            lanes = slice(start, start + tile)
-            act, slope = gelu_and_slope(upper[rows, lanes])
-            activated[rows, lanes] = act.astype(BF16)
-            slope_ref[rows, lanes] = slope.astype(BF16)
-
+    act, slope = gelu_and_slope(dot_nn(low, up[...]) + up_bias[...])
+    act = act.astype(BF16)
+    activated[...] = act
+    slope_ref[...] = slope.astype(BF16)
     wait(*range(1, 1 + len(downs)))
-    total = total + dot_nn(activated[...], down[...])
+    total = total + dot_nn(act, down[...])
     partial[...] = total
     partial_low[...] = total.astype(BF16)
 
@@ -493,8 +484,7 @@
          (weights["down"], "hbm"), (weights["dense"], "all")],
         [((rows, features), BF16, "rows")] + [((rows, units), BF16, "rows")] * 2
         + [((rows, features), F32, "rows"), ((rows, features), BF16, "rows")],
-        [pltpu.VMEM((features, units), BF16), pltpu.VMEM((units, features), BF16),
-         pltpu.VMEM((min(ROW_BLOCK, rows), units), F32)],
+        [pltpu.VMEM((features, units), BF16), pltpu.VMEM((units, features), BF16)],
         1 + sizes.down_copies, 2 * rows * features * (2 * units + width), "branches",
     )
 

time: 569 us -> 564 us (level)
  transfers between devices with their start and end apart: 45 -> 45, of which waited for: 21 -> 21; matrix products, arithmetic and copies ran while one was open for 12% -> 12% of each run, Pallas kernels for 20% -> 19%
where the time goes in v2:
time: 564 us; the launch traced here: 555 us
  waiting for transfers between devices  196 us (35%)
  Pallas kernels  170 us (30%)
  starting transfers between devices  63 us (11%)
  other arithmetic  44 us (8%)
  local copies, waits for them, and re-layouts  43.3 us (8%)
  matrix products  22.6 us (4%)
  between operations  16.5 us (3%)
    ppermute x29, waiting for transfers between devices, seq_shift(): lax.ppermute(array, 'seq', [(i, target(i) % count) for i in range(count)])  108 us
    pallas_call x8, Pallas kernels, row_call(): pl.pallas_call(functools.partial(kernel, sizes), grid=(rows // block,), i...  103 us
    ppermute x11, waiting for transfers between devices, cp_peer(): return lax.ppermute(array, 'cp', [(0, 1), (1, 0)])  83 us
    ppermute x29, starting transfers between devices, seq_shift(): lax.ppermute(array, 'seq', [(i, target(i) % count) for i in range(count)])  40.8 us
    pallas_call x2, Pallas kernels, attention_backward(): pl.pallas_call(backward_kernel, grid=(pairs,), in_specs=[column] * 5 + [s...  29.6 us
    pallas_call x2, Pallas kernels, attention_forward(): pl.pallas_call(forward_kernel, grid=(pairs,), in_specs=[column] * 3 + [wh...  22.8 us
    dot_general x8, matrix products, dot_tn(): lax.dot_general(left, right, (((0,), (0,)), ((), ())), preferred_element_...  22.6 us
    unnamed x169, local copies, waits for them, and re-layouts  20 us
  transfers between devices with their start and end apart: 45, of which 21 were waited for; matrix products, arithmetic and copies ran while one was open for 12% of the time, Pallas kernels for 19%

profile of v2, /device:TPU:1, one launch (start us, length us, event | category | flops | bytes accessed | tf_op | source)
XLA Modules:
  0.0 555.1 jit_solution(122419130052497917)
XLA Ops:
  15.2 13.0 %collective-permute-done.1 = s32[512]{0:T(512)S(1)} collective-permute-done((s32[512]{0:T(512)S(1)}, s32[512]{0:T(512)S(1)}, u32[]{:S(2)}, u32[]{:S(2)}) %collective-permute-start.1) | collective-permute-done | bytes 2080 | tf_op jit(solution)/shard_map/ppermute | solution.py:41
  56.4 12.1 %collective-permute-done.4 = bf16[48,4992]{1,0:T(8,128)(2,1)S(1)} collective-permute-done((bf16[48,4992]{1,0:T(8,128)(2,1)}, bf16[48,4992]{1,0:T(8,128)(2,1)S(1)}, u32[]{:S(2)}, u32[]{:S(2)}) %collective-permute-start.4) | collective-permute-done | bytes 479264 | tf_op jit(solution)/shard_map/ppermute | solution.py:100
  69.4 10.5 %collective-permute-done.5 = bf16[48,4992]{1,0:T(8,128)(2,1)S(1)} collective-permute-done((bf16[48,4992]{1,0:T(8,128)(2,1)S(1)}, bf16[48,4992]{1,0:T(8,128)(2,1)S(1)}, u32[]{:S(2)}, u32[]{:S(2)}) %collective-permute-start.5) | collective-permute-done | bytes 479264 | tf_op jit(solution)/shard_map/ppermute | solution.py:100
  90.8 14.4 %collective-permute-start.14 = (bf16[2,2,48,4992]{3,2,1,0:T(8,128)(2,1)S(1)}, bf16[2,2,48,4992]{3,2,1,0:T(8,128)(2,1)S(1)}, u32[]{:S(2)}, u32[]{:S(2)}) collective-permute-start(bf16[2,2,48,4992]{3,2,1,0:T(8,128)(2,1)S(1)} %get-tuple-element.203), channel_id=1, source_target_pairs={{0,2},{2,0},{4,6},{6,4},{8,10},{10,8},{12,14},{14,12},{16,18},{18,... | collective-permute-start | bytes 5750792 | tf_op jit(solution)/shard_map/ppermute | solution.py:100
  115.0 6.4 %collective-permute-start.17 = (bf16[2,2,48,4992]{3,2,1,0:T(8,128)(2,1)S(1)}, bf16[2,2,48,4992]{3,2,1,0:T(8,128)(2,1)S(1)}, u32[]{:S(2)}, u32[]{:S(2)}) collective-permute-start(bf16[2,2,48,4992]{3,2,1,0:T(8,128)(2,1)S(1)} %get-tuple-element.201), channel_id=1, source_target_pairs={{0,2},{2,0},{4,6},{6,4},{8,10},{10,8},{12,14},{14,12},{16,18},{18,... | collective-permute-start | bytes 5750792 | tf_op jit(solution)/shard_map/ppermute | solution.py:100
  129.6 7.0 %project.2 = (bf16[1024,768]{1,0:T(8,128)(2,1)S(1)}, bf16[1024,384]{1,0:T(8,128)(2,1)S(1)}, bf16[1024,384]{1,0:T(8,128)(2,1)S(1)}, bf16[1024,384]{1,0:T(8,128)(2,1)S(1)}) custom-call(f32[1024,768]{1,0:T(8,128)} %bitcast_convert_fusion.hidden, f32[1,768]{1,0:T(1,128)S(1)} %get-tuple-element.237.gain, f32[1,768]{1,0:T(1,128)S(1)} %get-tuple-element.236.bias, ...), custom_call_target="tpu_custom_call" | custom-call | flops 226492416 | bytes 786432 | tf_op jit(solution)/shard_map/project/pallas_call | solution.py:409
  137.8 11.4 %attention_forward.2 = (bf16[1024,384]{1,0:T(8,128)(2,1)S(1)}, f32[3,2,1024]{2,1,0:T(2,128)S(1)}) custom-call(bf16[1024,384]{1,0:T(8,128)(2,1)S(1)} %get-tuple-element.114.q_ref, bf16[1024,384]{1,0:T(8,128)(2,1)S(1)} %get-tuple-element.115.k_ref, bf16[1024,384]{1,0:T(8,128)(2,1)S(1)} %get-tuple-element.116.v_ref, bf16[1024,128]{1,0:T(8,128)(2,1)S(1)} %fusion.7.query_pen, ...), custom_call_target="tpu_custom_call" | custom-call | flops 402653184 | bytes 393216 | tf_op jit(solution)/shard_map/attention_forward/pallas_call | solution.py:225
  149.3 21.2 %branches.2 = (bf16[1024,768]{1,0:T(8,128)(2,1)S(1)}, bf16[1024,1536]{1,0:T(8,128)(2,1)}, bf16[1024,1536]{1,0:T(8,128)(2,1)}, f32[1024,768]{1,0:T(8,128)}, bf16[1024,768]{1,0:T(8,128)(2,1)}) custom-call(f32[1024,768]{1,0:T(8,128)} %bitcast_convert_fusion.hidden, bf16[1024,384]{1,0:T(8,128)(2,1)S(1)} %get-tuple-element.117.attended.out_ref, ...), custom_call_target="tpu_custom_call" | custom-call | flops 679477248 | bytes 786432 | tf_op jit(solution)/shard_map/branches/pallas_call | solution.py:409
  172.7 34.9 %collective-permute-done.18 = bf16[1024,768]{1,0:T(8,128)(2,1)} collective-permute-done((bf16[1024,768]{1,0:T(8,128)(2,1)}, bf16[1024,768]{1,0:T(8,128)(2,1)}, u32[]{:S(2)}, u32[]{:S(2)}) %collective-permute-start.18) | collective-permute-done | bytes 1572896 | tf_op jit(solution)/shard_map/ppermute | solution.py:41
  214.0 7.4 %project.3 = (bf16[1024,768]{1,0:T(8,128)(2,1)S(1)}, bf16[1024,384]{1,0:T(8,128)(2,1)S(1)}, bf16[1024,384]{1,0:T(8,128)(2,1)S(1)}, bf16[1024,384]{1,0:T(8,128)(2,1)S(1)}) custom-call(f32[1024,768]{1,0:T(8,128)} %add_add_fusion.1.hidden, f32[1,768]{1,0:T(1,128)S(1)} %get-tuple-element.231.gain, f32[1,768]{1,0:T(1,128)S(1)} %get-tuple-element.230.bias, ...), custom_call_target="tpu_custom_call" | custom-call | flops 226492416 | bytes 786432 | tf_op jit(solution)/shard_map/project/pallas_call | solution.py:409
  222.6 11.4 %attention_forward.3 = (bf16[1024,384]{1,0:T(8,128)(2,1)S(1)}, f32[3,2,1024]{2,1,0:T(2,128)S(1)}) custom-call(bf16[1024,384]{1,0:T(8,128)(2,1)S(1)} %get-tuple-element.121.q_ref, bf16[1024,384]{1,0:T(8,128)(2,1)S(1)} %get-tuple-element.122.k_ref, bf16[1024,384]{1,0:T(8,128)(2,1)S(1)} %get-tuple-element.123.v_ref, bf16[1024,128]{1,0:T(8,128)(2,1)S(1)} %fusion.7.query_pen, ...), custom_call_target="tpu_custom_call" | custom-call | flops 402653184 | bytes 393216 | tf_op jit(solution)/shard_map/attention_forward/pallas_call | solution.py:225
  234.0 21.0 %branches.3 = (bf16[1024,768]{1,0:T(8,128)(2,1)S(1)}, bf16[1024,1536]{1,0:T(8,128)(2,1)}, bf16[1024,1536]{1,0:T(8,128)(2,1)}, f32[1024,768]{1,0:T(8,128)}, bf16[1024,768]{1,0:T(8,128)(2,1)S(1)}) custom-call(f32[1024,768]{1,0:T(8,128)} %add_add_fusion.1.hidden, bf16[1024,384]{1,0:T(8,128)(2,1)S(1)} %get-tuple-element.124.attended.out_ref, ...), custom_call_target="tpu_custom_call" | custom-call | flops 679477248 | bytes 786432 | tf_op jit(solution)/shard_map/branches/pallas_call | solution.py:409
  261.1 14.0 %branches_back.2 = (bf16[1024,384]{1,0:T(8,128)(2,1)S(1)}, bf16[1024,1536]{1,0:T(8,128)(2,1)S(1)}, f32[1024,768]{1,0:T(8,128)}, f32[8,768]{1,0:T(8,128)S(1)}, f32[8,1536]{1,0:T(8,128)S(1)}) custom-call(bf16[1024,768]{1,0:T(8,128)(2,1)S(1)} %bitcast.163, bf16[1024,1536]{1,0:T(8,128)(2,1)} %get-tuple-element.128.slope, f32[1024,768]{1,0:T(8,128)} %add_add_fusion.1.hidden, ...), custom_call_target="tpu_custom_call" | custom-call | flops 679477248 | bytes 786432 | tf_op jit(solution)/shard_map/branches_back/pallas_call | solution.py:409
  290.3 14.7 %attention_backward.2.mixed = bf16[1024,1152]{1,0:T(8,128)(2,1)} custom-call(bf16[1024,384]{1,0:T(8,128)(2,1)S(1)} %copy-done.20, bf16[1024,384]{1,0:T(8,128)(2,1)S(1)} %copy-done.22, bf16[1024,384]{1,0:T(8,128)(2,1)S(1)} %copy-done.24, bf16[1024,384]{1,0:T(8,128)(2,1)S(1)} %copy-done.6, bf16[1024,384]{1,0:T(8,128)(2,1)S(1)} %copy-done.26, ...), custom_call_target="tpu_custom_call" | custom-call | flops 402653184 | bytes 393216 | tf_op jit(solution)/shard_map/attention_backward/pallas_call | solution.py:311
  306.6 9.4 %project_back.2 = (f32[1024,768]{1,0:T(8,128)}, bf16[1024,768]{1,0:T(8,128)(2,1)S(1)}, f32[8,768]{1,0:T(8,128)S(1)}, f32[8,1152]{1,0:T(8,128)S(1)}) custom-call(bf16[1024,1152]{1,0:T(8,128)(2,1)S(1)} %copy-done.2, f32[1024,768]{1,0:T(8,128)} %get-tuple-element.138.grad_mlp, f32[1024,768]{1,0:T(8,128)} %add_add_fusion.1.hidden, ...), custom_call_target="tpu_custom_call" | custom-call | flops 226492416 | bytes 786432 | tf_op jit(solution)/shard_map/project_back/pallas_call | solution.py:409
  319.4 31.0 %collective-permute-done.20 = bf16[1024,768]{1,0:T(8,128)(2,1)S(1)} collective-permute-done((bf16[1024,768]{1,0:T(8,128)(2,1)S(1)}, bf16[1024,768]{1,0:T(8,128)(2,1)S(1)}, u32[]{:S(2)}, u32[]{:S(2)}) %collective-permute-start.20) | collective-permute-done | bytes 1572896 | tf_op jit(solution)/shard_map/ppermute | solution.py:41
  352.8 13.9 %branches_back.3 = (bf16[1024,384]{1,0:T(8,128)(2,1)S(1)}, bf16[1024,1536]{1,0:T(8,128)(2,1)S(1)}, f32[1024,768]{1,0:T(8,128)}, f32[8,768]{1,0:T(8,128)S(1)}, f32[8,1536]{1,0:T(8,128)S(1)}) custom-call(bf16[1024,768]{1,0:T(8,128)(2,1)S(1)} %get-tuple-element.190.low_ref, bf16[1024,1536]{1,0:T(8,128)(2,1)} %get-tuple-element.147.slope, ...), custom_call_target="tpu_custom_call" | custom-call | flops 679477248 | bytes 786432 | tf_op jit(solution)/shard_map/branches_back/pallas_call | solution.py:409
  375.5 7.4 %pack_terms.2 = bf16[4,2,48,4992]{3,2,1,0:T(8,128)(2,1)} custom-call(s32[3]{0:T(128)S(1)} %pad_add_fusion.1.place, bf16[768,1536]{1,0:T(8,128)(2,1)S(1)} %convolution_convert_fusion.1.refs_0_.refs_4_, bf16[1536,768]{1,0:T(8,128)(2,1)} %convolution_convert_fusion.refs_1_.refs_5_, bf16[768,768]{1,0:T(8,128)(2,1)S(1)} %fusion.1.refs_2_.refs_6_, ...), custom_call_target="tpu_custom_call" | custom-call | bytes 15335424 | tf_op jit(solution)/shard_map/pack_terms/pallas_call | solution.py:654
  385.7 14.9 %attention_backward.3.mixed = bf16[1024,1152]{1,0:T(8,128)(2,1)} custom-call(bf16[1024,384]{1,0:T(8,128)(2,1)S(1)} %copy-done.14, bf16[1024,384]{1,0:T(8,128)(2,1)S(1)} %copy-done.16, bf16[1024,384]{1,0:T(8,128)(2,1)S(1)} %copy-done.18, bf16[1024,384]{1,0:T(8,128)(2,1)S(1)} %copy-done.4, bf16[1024,384]{1,0:T(8,128)(2,1)S(1)} %get-tuple-element.156.grad_ref, ...), custom_call_target="tpu_custom_call" | custom-call | flops 402653184 | bytes 393216 | tf_op jit(solution)/shard_map/attention_backward/pallas_call | solution.py:311
  408.9 9.1 %project_back.3 = (f32[1024,768]{1,0:T(8,128)}, bf16[1024,768]{1,0:T(8,128)(2,1)S(1)}, f32[8,768]{1,0:T(8,128)S(1)}, f32[8,1152]{1,0:T(8,128)S(1)}) custom-call(bf16[1024,1152]{1,0:T(8,128)(2,1)S(1)} %copy-done.1, f32[1024,768]{1,0:T(8,128)} %get-tuple-element.164.grad_mlp, f32[1024,768]{1,0:T(8,128)} %bitcast_convert_fusion.hidden, ...), custom_call_target="tpu_custom_call" | custom-call | flops 226492416 | bytes 786432 | tf_op jit(solution)/shard_map/project_back/pallas_call | solution.py:409
  430.2 21.9 %collective-permute-done.25 = f32[2,9216]{1,0:T(2,128)S(1)} collective-permute-done((f32[2,9216]{1,0:T(2,128)S(1)}, f32[2,9216]{1,0:T(2,128)S(1)}, u32[]{:S(2)}, u32[]{:S(2)}) %collective-permute-start.25) | collective-permute-done | bytes 73760 | tf_op jit(solution)/shard_map/ppermute | solution.py:100
  479.8 12.5 %collective-permute-done.30 = bf16[48,4992]{1,0:T(8,128)(2,1)S(1)} collective-permute-done((bf16[48,4992]{1,0:T(8,128)(2,1)S(1)}, bf16[48,4992]{1,0:T(8,128)(2,1)S(1)}, u32[]{:S(2)}, u32[]{:S(2)}) %collective-permute-start.30) | collective-permute-done | bytes 479264 | tf_op jit(solution)/shard_map/ppermute | solution.py:100
  494.5 15.1 %collective-permute-done.36 = bf16[48,1152]{1,0:T(8,128)(2,1)S(1)} collective-permute-done((bf16[48,1152]{1,0:T(8,128)(2,1)S(1)}, bf16[48,1152]{1,0:T(8,128)(2,1)S(1)}, u32[]{:S(2)}, u32[]{:S(2)}) %collective-permute-start.36) | collective-permute-done | bytes 110624 | tf_op jit(solution)/shard_map/ppermute | solution.py:100
  518.1 9.1 %collective-permute-done.38 = bf16[48,1152]{1,0:T(8,128)(2,1)S(1)} collective-permute-done((bf16[48,1152]{1,0:T(8,128)(2,1)S(1)}, bf16[48,1152]{1,0:T(8,128)(2,1)S(1)}, u32[]{:S(2)}, u32[]{:S(2)}) %collective-permute-start.38) | collective-permute-done | bytes 110624 | tf_op jit(solution)/shard_map/ppermute | solution.py:100
  (428 shorter events, 195.0 us)
Async XLA Ops:
  7.2 205.4 %all-gather.2.cloned.1.call-start = ((), (), s32[]{:S(2)}) async-start(), calls=%async_computation.1 | async-start | bytes 8146944 | tf_op jit(solution)/shard_map/all_gather | solution.py:874
  7.2 21.0 %collective-permute-start.2 = (bf16[2,96,768]{2,1,0:T(8,128)(2,1)}, bf16[2,96,768]{2,1,0:T(8,128)(2,1)S(1)}, u32[]{:S(2)}, u32[]{:S(2)}) collective-permute-start(bf16[2,96,768]{2,1,0:T(8,128)(2,1)} %param.28), channel_id=1, source_target_pairs={{0,0},{1,2},{2,4},{3,6},{4,8},{5,10},{6,12},{7,14},{8,16},{9,18},{... | collective-permute-start | bytes 884744 | tf_op jit(solution)/shard_map/ppermute | solution.py:839
  13.6 15.0 %collective-permute-start = (bf16[2,24,3456]{2,1,0:T(8,128)(2,1)S(1)}, bf16[2,24,3456]{2,1,0:T(8,128)(2,1)S(1)}, u32[]{:S(2)}, u32[]{:S(2)}) collective-permute-start(bf16[2,24,3456]{2,1,0:T(8,128)(2,1)S(1)} %fusion.14), channel_id=1, source_target_pairs={{0,1},{1,0},{2,3},{3,2},{4,5},{5,4},{6,7},{7,6},{8,9},{9,8},{10,11... | collective-permute-start | bytes 995336 | tf_op jit(solution)/shard_map/ppermute | solution.py:41
  30.1 26.0 %collective-permute-start.3 = (bf16[48,4992]{1,0:T(8,128)(2,1)}, bf16[48,4992]{1,0:T(8,128)(2,1)}, u32[]{:S(2)}, u32[]{:S(2)}) collective-permute-start(bf16[48,4992]{1,0:T(8,128)(2,1)} %get-tuple-element.213), channel_id=1, source_target_pairs={{0,8},{2,10},{4,12},{6,14},{8,16},{10,18},{12,20},{14,22},{16,24},... | collective-permute-start | bytes 1437704 | tf_op jit(solution)/shard_map/ppermute | solution.py:100
  30.1 50.2 %collective-permute-start.12 = (bf16[48,4992]{1,0:T(8,128)(2,1)}, bf16[48,4992]{1,0:T(8,128)(2,1)}, u32[]{:S(2)}, u32[]{:S(2)}) collective-permute-start(bf16[48,4992]{1,0:T(8,128)(2,1)} %get-tuple-element.213), channel_id=1, source_target_pairs={{0,4},{2,6},{4,0},{6,2},{8,12},{10,14},{12,8},{14,10},{16,20},{18,... | collective-permute-start | bytes 1437704 | tf_op jit(solution)/shard_map/ppermute | solution.py:100
  38.3 41.6 %collective-permute-start.6 = (bf16[2,512,768]{2,1,0:T(8,128)(2,1)}, bf16[2,512,768]{2,1,0:T(8,128)(2,1)}, u32[]{:S(2)}, u32[]{:S(2)}) collective-permute-start(bf16[2,512,768]{2,1,0:T(8,128)(2,1)} %pad_maximum_fusion.4), channel_id=1, source_target_pairs={{0,1},{1,0},{2,3},{3,2},{4,5},{5,4},{6,7},{7,6},{8,9},{9,8},{10,11... | collective-permute-start | bytes 4718600 | tf_op jit(solution)/shard_map/ppermute | solution.py:41
  79.9 328.0 %reduce-scatter.2.cloned.1.call-start = ((), (), s32[]{:S(2)}) async-start(), calls=%async_computation.2 | async-start | bytes 6266880 | tf_op jit(solution)/shard_map/reduce_scatter | solution.py:949
  82.1 23.1 %collective-permute-start.15 = (bf16[48,4992]{1,0:T(8,128)(2,1)S(1)}, bf16[48,4992]{1,0:T(8,128)(2,1)S(1)}, u32[]{:S(2)}, u32[]{:S(2)}) collective-permute-start(bf16[48,4992]{1,0:T(8,128)(2,1)S(1)} %copy-done.52), channel_id=1, source_target_pairs={{0,4},{2,6},{4,0},{6,2},{8,12},{10,14},{12,8},{14,10},{16,20},{18,... | collective-permute-start | bytes 1437704 | tf_op jit(solution)/shard_map/ppermute | solution.py:100
  90.8 30.6 %collective-permute-start.14 = (bf16[2,2,48,4992]{3,2,1,0:T(8,128)(2,1)S(1)}, bf16[2,2,48,4992]{3,2,1,0:T(8,128)(2,1)S(1)}, u32[]{:S(2)}, u32[]{:S(2)}) collective-permute-start(bf16[2,2,48,4992]{3,2,1,0:T(8,128)(2,1)S(1)} %get-tuple-element.203), channel_id=1, source_target_pairs={{0,2},{2,0},{4,6},{6,4},{8,10},{10,8},{12,14},{14,12},{16,18},{18,... | collective-permute-start | bytes 5750792 | tf_op jit(solution)/shard_map/ppermute | solution.py:100
  171.7 35.9 %collective-permute-start.18 = (bf16[1024,768]{1,0:T(8,128)(2,1)}, bf16[1024,768]{1,0:T(8,128)(2,1)}, u32[]{:S(2)}, u32[]{:S(2)}) collective-permute-start(bf16[1024,768]{1,0:T(8,128)(2,1)} %get-tuple-element.119), channel_id=1, source_target_pairs={{0,1},{1,0},{2,3},{3,2},{4,5},{5,4},{6,7},{7,6},{8,9},{9,8},{10,11... | collective-permute-start | bytes 4718600 | tf_op jit(solution)/shard_map/ppermute | solution.py:41
  316.0 34.4 %collective-permute-start.20 = (bf16[1024,768]{1,0:T(8,128)(2,1)S(1)}, bf16[1024,768]{1,0:T(8,128)(2,1)S(1)}, u32[]{:S(2)}, u32[]{:S(2)}) collective-permute-start(bf16[1024,768]{1,0:T(8,128)(2,1)S(1)} %get-tuple-element.143), channel_id=1, source_target_pairs={{0,1},{1,0},{2,3},{3,2},{4,5},{5,4},{6,7},{7,6},{8,9},{9,8},{10,11... | collective-permute-start | bytes 4718600 | tf_op jit(solution)/shard_map/ppermute | solution.py:41
  382.9 17.7 %collective-permute-start.21 = (bf16[4,2,48,4992]{3,2,1,0:T(8,128)(2,1)}, bf16[4,2,48,4992]{3,2,1,0:T(8,128)(2,1)}, u32[]{:S(2)}, u32[]{:S(2)}) collective-permute-start(bf16[4,2,48,4992]{3,2,1,0:T(8,128)(2,1)} %pack_terms.2), channel_id=1, source_target_pairs={{0,2},{2,0},{4,6},{6,4},{8,10},{10,8},{12,14},{14,12},{16,18},{18,... | collective-permute-start | bytes 11501576 | tf_op jit(solution)/shard_map/ppermute | solution.py:100
  425.5 26.7 %collective-permute-start.19 = (bf16[512,768]{1,0:T(8,128)(2,1)S(1)}, bf16[512,768]{1,0:T(8,128)(2,1)S(1)}, u32[]{:S(2)}, u32[]{:S(2)}) collective-permute-start(bf16[512,768]{1,0:T(8,128)(2,1)S(1)} %constant_dynamic-slice_fusion.8), channel_id=1, source_target_pairs={{0,1},{1,0},{2,3},{3,2},{4,5},{5,4},{6,7},{7,6},{8,9},{9,8},{10,11... | collective-permute-start | bytes 2359304 | tf_op jit(solution)/shard_map/ppermute | solution.py:41
  426.5 50.2 %collective-permute-start.29 = (bf16[2,48,4992]{2,1,0:T(8,128)(2,1)}, bf16[2,48,4992]{2,1,0:T(8,128)(2,1)}, u32[]{:S(2)}, u32[]{:S(2)}) collective-permute-start(bf16[2,48,4992]{2,1,0:T(8,128)(2,1)} %get-tuple-element.181), channel_id=1, source_target_pairs={{0,4},{2,6},{4,0},{6,2},{8,12},{10,14},{12,8},{14,10},{16,20},{18,... | collective-permute-start | bytes 2875400 | tf_op jit(solution)/shard_map/ppermute | solution.py:100
  428.9 23.2 %collective-permute-start.25 = (f32[2,9216]{1,0:T(2,128)S(1)}, f32[2,9216]{1,0:T(2,128)S(1)}, u32[]{:S(2)}, u32[]{:S(2)}) collective-permute-start(f32[2,9216]{1,0:T(2,128)S(1)} %fusion.64), channel_id=1, source_target_pairs={{0,4},{2,6},{4,0},{6,2},{8,12},{10,14},{12,8},{14,10},{16,20},{18,... | collective-permute-start | bytes 221192 | tf_op jit(solution)/shard_map/ppermute | solution.py:100
  429.9 45.1 %collective-permute-start.22 = (bf16[512,768]{1,0:T(8,128)(2,1)}, bf16[512,768]{1,0:T(8,128)(2,1)}, u32[]{:S(2)}, u32[]{:S(2)}) collective-permute-start(bf16[512,768]{1,0:T(8,128)(2,1)} %constant_dynamic-slice_fusion.7), channel_id=1, source_target_pairs={{0,1},{1,0},{2,3},{3,2},{4,5},{5,4},{6,7},{7,6},{8,9},{9,8},{10,11... | collective-permute-start | bytes 2359304 | tf_op jit(solution)/shard_map/ppermute | solution.py:41
  456.1 53.5 %collective-permute-start.28 = (bf16[2,48,4992]{2,1,0:T(8,128)(2,1)}, bf16[2,48,4992]{2,1,0:T(8,128)(2,1)}, u32[]{:S(2)}, u32[]{:S(2)}) collective-permute-start(bf16[2,48,4992]{2,1,0:T(8,128)(2,1)} %get-tuple-element.180), channel_id=1, source_target_pairs={{0,4},{2,6},{4,0},{6,2},{8,12},{10,14},{12,8},{14,10},{16,20},{18,... | collective-permute-start | bytes 2875400 | tf_op jit(solution)/shard_map/ppermute | solution.py:100
  457.9 77.8 %collective-permute-start.42 = (bf16[96,768]{1,0:T(8,128)(2,1)}, bf16[96,768]{1,0:T(8,128)(2,1)}, u32[]{:S(2)}, u32[]{:S(2)}) collective-permute-start(bf16[96,768]{1,0:T(8,128)(2,1)} %bitcast.66), channel_id=1, source_target_pairs={{0,0},{2,1},{4,2},{6,3},{8,4},{10,5},{12,6},{14,7},{16,8},{18,9},{... | collective-permute-start | bytes 442376 | tf_op jit(solution)/shard_map/ppermute | solution.py:839
  477.9 14.4 %collective-permute-start.30 = (bf16[48,4992]{1,0:T(8,128)(2,1)S(1)}, bf16[48,4992]{1,0:T(8,128)(2,1)S(1)}, u32[]{:S(2)}, u32[]{:S(2)}) collective-permute-start(bf16[48,4992]{1,0:T(8,128)(2,1)S(1)} %fusion.8), channel_id=1, source_target_pairs={{0,8},{2,10},{4,12},{6,14},{8,16},{10,18},{12,20},{14,22},{16,24},... | collective-permute-start | bytes 1437704 | tf_op jit(solution)/shard_map/ppermute | solution.py:100
  479.7 14.0 %collective-permute-start.35 = (bf16[2,48,1152]{2,1,0:T(8,128)(2,1)S(1)}, bf16[2,48,1152]{2,1,0:T(8,128)(2,1)S(1)}, u32[]{:S(2)}, u32[]{:S(2)}) collective-permute-start(bf16[2,48,1152]{2,1,0:T(8,128)(2,1)S(1)} %get-tuple-element.215), channel_id=1, source_target_pairs={{0,4},{2,6},{4,0},{6,2},{8,12},{10,14},{12,8},{14,10},{16,20},{18,... | collective-permute-start | bytes 663560 | tf_op jit(solution)/shard_map/ppermute | solution.py:100
  493.6 16.0 %collective-permute-start.31 = (bf16[48,4992]{1,0:T(8,128)(2,1)S(1)}, bf16[48,4992]{1,0:T(8,128)(2,1)S(1)}, u32[]{:S(2)}, u32[]{:S(2)}) collective-permute-start(bf16[48,4992]{1,0:T(8,128)(2,1)S(1)} %fusion.3), channel_id=1, source_target_pairs={{0,8},{2,10},{4,12},{6,14},{8,16},{10,18},{12,20},{14,22},{16,24},... | collective-permute-start | bytes 1437704 | tf_op jit(solution)/shard_map/ppermute | solution.py:100
  493.7 15.8 %collective-permute-start.36 = (bf16[48,1152]{1,0:T(8,128)(2,1)S(1)}, bf16[48,1152]{1,0:T(8,128)(2,1)S(1)}, u32[]{:S(2)}, u32[]{:S(2)}) collective-permute-start(bf16[48,1152]{1,0:T(8,128)(2,1)S(1)} %fusion.30), channel_id=1, source_target_pairs={{0,8},{2,10},{4,12},{6,14},{8,16},{10,18},{12,20},{14,22},{16,24},... | collective-permute-start | bytes 331784 | tf_op jit(solution)/shard_map/ppermute | solution.py:100
  494.5 16.4 %collective-permute-start.34 = (bf16[2,48,1152]{2,1,0:T(8,128)(2,1)S(1)}, bf16[2,48,1152]{2,1,0:T(8,128)(2,1)S(1)}, u32[]{:S(2)}, u32[]{:S(2)}) collective-permute-start(bf16[2,48,1152]{2,1,0:T(8,128)(2,1)S(1)} %get-tuple-element.214), channel_id=1, source_target_pairs={{0,4},{2,6},{4,0},{6,2},{8,12},{10,14},{12,8},{14,10},{16,20},{18,... | collective-permute-start | bytes 663560 | tf_op jit(solution)/shard_map/ppermute | solution.py:100
  510.8 16.4 %collective-permute-start.32 = (bf16[48,4992]{1,0:T(8,128)(2,1)S(1)}, bf16[48,4992]{1,0:T(8,128)(2,1)S(1)}, u32[]{:S(2)}, u32[]{:S(2)}) collective-permute-start(bf16[48,4992]{1,0:T(8,128)(2,1)S(1)} %fusion.4), channel_id=1, source_target_pairs={{0,8},{2,10},{4,12},{6,14},{8,16},{10,18},{12,20},{14,22},{16,24},... | collective-permute-start | bytes 1437704 | tf_op jit(solution)/shard_map/ppermute | solution.py:100
  (90 other events, 833.5 us)
Sparse Core Ops, SparseCore 0:
  80.1 74.5 all-gather.1
  283.7 81.4 reduce-scatter.1
